TPU v7x, 32 devices: a whole 2x2x4 slice. The times are simulated.
32 devices in a mesh: shot: 4 (over x, core), beam: 8 (over z, y).
Axes of the slice: x: 2, y: 2, z: 4, core: 2. Of those that a mesh axis runs over, the one named last changes fastest.
Arguments:
- traces: bfloat16 [4, 2048, 128], P('shot', 'beam'), may hold values from -6 to 6
- send_table: int32 [4, 8, 8, 32], P('shot'), may hold values from 0 to 255
- window_slots: int32 [4, 64, 32], P('shot', 'beam'), may hold values from 0 to 255
- ray_depth: float32 [4, 2048, 32, 128], P('shot', 'beam'), may hold values from 0 to 0.25
- ray_lateral: float32 [2048, 32, 128], P('beam'), may hold values from 0 to 0.25
- ray_spread: float32 [2048, 32, 128], P('beam'), may hold values from 0.0001 to 0.004
- ray_index: int32 [64, 12], P('beam'), may hold values from 0 to 255
- foot_count: int32 [8, 8], P('beam'), may hold values from 1 to 12, 80 in all within a row
- foot_tiles: int32 [64, 12], replicated, may hold values from 0 to 127, as said below
- tile_owner: int32 [128], replicated, may hold values from 0 to 31, as said below
Outputs:
- image_tiles: float32 [128, 128, 128], P(('shot', 'beam'))
Inputs may be any that keep to these rules, and one draw needn't show every extreme that they name: `send_table`: entry [s, j, g, i] is a row among the traces of shot gather s held by beam index j. `window_slots`: a slot of the block that the centre's group received, numbered source by source. `ray_index`: a row within the ray table of the centre's group. `foot_count`: the 8 counts of each group sum to 80. `foot_tiles`: entries past a centre's count hold tiles too; one centre's entries have distinct owners; within one group, entries whose tiles have the same owner name the same tile. `tile_owner`: each owner holds exactly 4 tiles.
All inputs are finite; a program needn't handle non-finite values.
Results may differ from a plain program's by a relative error of at most 0.0048.
Values may be sent and summed in bfloat16 or wider, within the bound.
No kernel may reach another device: no remote copies, remote signals or barrier semaphores. Data moves between devices by JAX's collectives and lax.ppermute only.
A program may use at most 192 MiB of HBM per device.

v0:
```python
import math

import jax
import jax.numpy as jnp
from jax import lax
from jax.sharding import PartitionSpec as P

FREQUENCIES = 64
DIRECTIONS = 32
WINDOW = 32


def slant_tables():
    freq_index = jnp.arange(FREQUENCIES, dtype=jnp.float32)
    angular = 2.0 * math.pi * (4.0 + 60.0 * freq_index / FREQUENCIES)
    centred = jnp.arange(WINDOW, dtype=jnp.float32) - 0.5 * (WINDOW - 1)
    taper_weight = jnp.exp(-((centred / (0.25 * WINDOW)) ** 2)) / math.sqrt(WINDOW)
    slowness = 2e-05 * (jnp.arange(DIRECTIONS, dtype=jnp.float32) - 0.5 * (DIRECTIONS - 1))
    stack_angle = angular[:, None, None] * slowness[None, :, None] * (25.0 * centred)[None, None, :]
    stack_real = (taper_weight * jnp.cos(stack_angle)).astype(jnp.bfloat16)
    stack_imag = (-taper_weight * jnp.sin(stack_angle)).astype(jnp.bfloat16)
    return (angular, stack_real, stack_imag)


def pair_factors(
    beam_real, beam_imag, depth_times, lateral_times, spread_rates, live_mask, angular
):
    direction_count = beam_real.shape[1]
    freq_count = beam_real.shape[2]
    pair_count = depth_times.shape[0]
    weight_scale = (live_mask / math.sqrt(direction_count * freq_count))[:, None, None, None]
    depth_phase = angular[None, None, :, None] * depth_times[:, :, None, :]
    depth_cos = jnp.cos(depth_phase)
    depth_sin = jnp.sin(depth_phase)
    part_real = (beam_real[..., None] * depth_cos - beam_imag[..., None] * depth_sin) * weight_scale
    part_imag = (beam_real[..., None] * depth_sin + beam_imag[..., None] * depth_cos) * weight_scale
    depth_factor = jnp.stack([part_real, -part_imag], axis=1).astype(jnp.bfloat16)
    lateral_phase = angular[None, None, :, None] * lateral_times[:, :, None, :]
    damping = jnp.exp(-angular[None, None, :, None] * spread_rates[:, :, None, :])
    lateral_factor = jnp.stack(
        [damping * jnp.cos(lateral_phase), damping * jnp.sin(lateral_phase)], axis=1
    ).astype(jnp.bfloat16)
    depth_factor = depth_factor.reshape(
        pair_count, 2 * direction_count * freq_count, depth_times.shape[2]
    )
    lateral_factor = lateral_factor.reshape(
        pair_count, 2 * direction_count * freq_count, lateral_times.shape[2]
    )
    return (depth_factor, lateral_factor)


def group_slots(foot_tiles, tile_owner, tile_slot, groups, owner_id):
    group_tiles = foot_tiles.reshape(groups, -1)
    return jnp.max(
        jnp.where(tile_owner[group_tiles] == owner_id, tile_slot[group_tiles], 0), axis=1
    )


def body(
    traces,
    send_table,
    window_slots,
    ray_depth,
    ray_lateral,
    ray_spread,
    ray_index,
    foot_count,
    foot_tiles,
    tile_owner,
):
    groups = lax.axis_size("beam")
    shot_count = lax.axis_size("shot")
    group_id = lax.axis_index("beam")
    owner_id = lax.axis_index("shot") * groups + group_id
    owner_count = shot_count * groups
    angular, stack_real, stack_imag = slant_tables()
    trace_rows = traces[0]
    trace_dev = trace_rows.shape[0]
    routes = send_table[0]
    all_rows = lax.all_gather(trace_rows, "beam", axis=0, tiled=True)
    my_routes = lax.dynamic_index_in_dim(routes, group_id, 1, keepdims=False)
    flat_index = (jnp.arange(groups, dtype=jnp.int32)[:, None] * trace_dev + my_routes).reshape(-1)
    arrived = all_rows[flat_index]
    slot_table = window_slots[0]
    centre_count = slot_table.shape[0]
    window = slot_table.shape[1]
    windows = arrived[slot_table.reshape(-1)].reshape(centre_count, window, -1)
    freq_count = angular.shape[0]
    trace_real = windows[..., :freq_count]
    trace_imag = windows[..., freq_count:]
    beam_real = jnp.einsum(
        "fpk,ckf->cpf", stack_real, trace_real, preferred_element_type=jnp.float32
    ) - jnp.einsum("fpk,ckf->cpf", stack_imag, trace_imag, preferred_element_type=jnp.float32)
    beam_imag = jnp.einsum(
        "fpk,ckf->cpf", stack_real, trace_imag, preferred_element_type=jnp.float32
    ) + jnp.einsum("fpk,ckf->cpf", stack_imag, trace_real, preferred_element_type=jnp.float32)
    foot_slots = ray_index.shape[1]
    entries = centre_count * foot_slots
    entry_ids = jnp.arange(entries, dtype=jnp.int32)
    centre_local = entry_ids // foot_slots
    slot_local = entry_ids % foot_slots
    alive_flag = (slot_local < foot_count[0][centre_local]).astype(jnp.int32)
    ray_rows = ray_index.reshape(-1)
    my_tiles = lax.dynamic_slice_in_dim(
        foot_tiles, group_id * centre_count, centre_count, 0
    ).reshape(-1)
    entry_owner = tile_owner[my_tiles]
    depth_table = ray_depth[0]
    depth_cells = depth_table.shape[2]
    lateral_cells = ray_lateral.shape[2]

    def one_block(buffer, chosen):
        centres = centre_local[chosen]
        rows_now = ray_rows[chosen]
        depth_factor, lateral_factor = pair_factors(
            beam_real[centres],
            beam_imag[centres],
            depth_table[rows_now],
            ray_lateral[rows_now],
            ray_spread[rows_now],
            alive_flag[chosen].astype(jnp.float32),
            angular,
        )
        contribution = jnp.einsum(
            "brz,brx->bzx", depth_factor, lateral_factor, preferred_element_type=jnp.float32
        )
        return (buffer.at[entry_owner[chosen]].add(contribution), None)

    buffer_start = jnp.zeros((owner_count, depth_cells, lateral_cells), jnp.float32)
    buffer, _ = lax.scan(one_block, buffer_start, entry_ids.reshape(-1, 8))
    tile_count = tile_owner.shape[0]
    tiles_each = tile_count // owner_count
    tile_order = jnp.argsort(tile_owner, stable=True)
    tile_rank = (
        jnp.zeros((tile_count,), jnp.int32)
        .at[tile_order]
        .set(jnp.arange(tile_count, dtype=jnp.int32))
    )
    tile_slot = tile_rank % tiles_each
    slot_range = jnp.arange(tiles_each, dtype=jnp.int32)
    highest = lax.Precision.HIGHEST
    group_slot = group_slots(foot_tiles, tile_owner, tile_slot, groups, owner_id)
    shared = lax.psum_scatter(
        buffer.reshape(shot_count, groups, depth_cells, lateral_cells),
        "shot",
        scatter_dimension=0,
        tiled=True,
    )
    received = lax.all_to_all(
        shared.reshape(groups, depth_cells, lateral_cells),
        "beam",
        split_axis=0,
        concat_axis=0,
        tiled=True,
    )
    placed = (group_slot[:, None] == slot_range[None, :]).astype(jnp.float32)
    image_part = jnp.einsum("sj,szx->jzx", placed, received, precision=highest)
    return image_part


def solution(mesh):
    in_specs = (
        P("shot", "beam", None),
        P("shot", None, None, None),
        P("shot", "beam", None),
        P("shot", "beam", None, None),
        P("beam", None, None),
        P("beam", None, None),
        P("beam", None),
        P("beam", None),
        P(),
        P(),
    )
    out_specs = P(("shot", "beam"), None, None)
    return jax.shard_map(body, mesh=mesh, in_specs=in_specs, out_specs=out_specs, check_vma=False)
```

profile of v0, /device:TPU:0, one launch (start us, length us, event | category | flops | bytes accessed | tf_op | source)
XLA Modules:
  0.0 1286.7 jit_solution(13671107420660279672)
XLA Ops:
  11.0 33.2 %all-gather = bf16[1,2048,128]{2,1,0:T(8,128)(2,1)S(1)} all-gather(bf16[1,256,128]{2,1,0:T(8,128)(2,1)} %param.12), channel_id=2, replica_groups=mesh['shot'=4,'beam'=8] {'beam'}, dimensions={1}, use_global_device_ids=true | all-gather | bytes 589824 | tf_op jit(solution)/shard_map/all_gather | solution.py:80
  46.4 3.6 fusion.38
  50.0 3.6 fusion.36
  53.6 3.7 fusion.29
  57.7 3.6 fusion.28
  63.3 1160.9 %while.13 = (s32[]{:T(128)}, f32[32,128,128]{2,1,0:T(8,128)S(1)}, s32[12,8]{1,0:T(8,128)S(1)}, s32[96]{0:T(128)S(1)}, f32[8,32,64]{2,1,0:T(8,128)S(1)}, /*index=...) while((s32[]{:T(128)}, f32[32,128,128]{2,1,0:T(8,128)S(1)}, ...), condition=%wide.region_5.6_spmd.clone.clone, body=%wide.region_3.5_spmd.clone.clone.sunk | while | flops 1120017792 | bytes 70794200 | solution.py:130
  77.4 5.0 compare_convert_fusion.2
  86.2 2.7 gather_fusion.7
  94.5 63.0 %fusion.87 = (bf16[8,1,32,64,128]{4,3,2,1,0:T(8,128)(2,1)S(1)}, bf16[8,1,32,64,128]{4,3,2,1,0:T(8,128)(2,1)S(1)}, bf16[8,1,32,64,128]{4,3,2,1,0:T(8,128)(2,1)S(1)}, bf16[8,1,32,64,128]{4,3,2,1,0:T(8,128)(2,1)S(1)}) fusion(f32[8,32,128]{2,1,0:T(8,128)S(1)} %gather_fusion.2, f32[8,32,128]{2,1,0:T(8,128)S(1)} %gather_fusion.3, ...), kind=kLoop, calls=%fused_computation.36.clone.1 | loop fusion | flops 37748736 | bytes 17302048 | tf_op jit(solution)/shard_map/convert
  157.4 6.1 pad_maximum_fusion.3
  163.5 8.3 fusion.88
  172.9 5.0 compare_convert_fusion.2
  184.5 2.7 gather_fusion.3
  187.3 2.7 gather_fusion.2
  190.0 63.0 %fusion.87 = (bf16[8,1,32,64,128]{4,3,2,1,0:T(8,128)(2,1)S(1)}, bf16[8,1,32,64,128]{4,3,2,1,0:T(8,128)(2,1)S(1)}, bf16[8,1,32,64,128]{4,3,2,1,0:T(8,128)(2,1)S(1)}, bf16[8,1,32,64,128]{4,3,2,1,0:T(8,128)(2,1)S(1)}) fusion(f32[8,32,128]{2,1,0:T(8,128)S(1)} %gather_fusion.2, f32[8,32,128]{2,1,0:T(8,128)S(1)} %gather_fusion.3, ...), kind=kLoop, calls=%fused_computation.36.clone.1 | loop fusion | flops 37748736 | bytes 17302048 | tf_op jit(solution)/shard_map/convert
  253.0 6.1 pad_maximum_fusion.3
  259.1 8.3 fusion.88
  268.5 5.0 compare_convert_fusion.2
  277.3 2.7 gather_fusion.7
  280.1 2.7 gather_fusion.3
  285.6 63.0 %fusion.87 = (bf16[8,1,32,64,128]{4,3,2,1,0:T(8,128)(2,1)S(1)}, bf16[8,1,32,64,128]{4,3,2,1,0:T(8,128)(2,1)S(1)}, bf16[8,1,32,64,128]{4,3,2,1,0:T(8,128)(2,1)S(1)}, bf16[8,1,32,64,128]{4,3,2,1,0:T(8,128)(2,1)S(1)}) fusion(f32[8,32,128]{2,1,0:T(8,128)S(1)} %gather_fusion.2, f32[8,32,128]{2,1,0:T(8,128)S(1)} %gather_fusion.3, ...), kind=kLoop, calls=%fused_computation.36.clone.1 | loop fusion | flops 37748736 | bytes 17302048 | tf_op jit(solution)/shard_map/convert
  348.5 6.1 pad_maximum_fusion.3
  354.6 8.3 fusion.88
  364.0 5.0 compare_convert_fusion.2
  381.1 63.0 %fusion.87 = (bf16[8,1,32,64,128]{4,3,2,1,0:T(8,128)(2,1)S(1)}, bf16[8,1,32,64,128]{4,3,2,1,0:T(8,128)(2,1)S(1)}, bf16[8,1,32,64,128]{4,3,2,1,0:T(8,128)(2,1)S(1)}, bf16[8,1,32,64,128]{4,3,2,1,0:T(8,128)(2,1)S(1)}) fusion(f32[8,32,128]{2,1,0:T(8,128)S(1)} %gather_fusion.2, f32[8,32,128]{2,1,0:T(8,128)S(1)} %gather_fusion.3, ...), kind=kLoop, calls=%fused_computation.36.clone.1 | loop fusion | flops 37748736 | bytes 17302048 | tf_op jit(solution)/shard_map/convert
  444.1 6.1 pad_maximum_fusion.3
  450.2 8.3 fusion.88
  459.6 5.0 compare_convert_fusion.2
  476.7 63.0 %fusion.87 = (bf16[8,1,32,64,128]{4,3,2,1,0:T(8,128)(2,1)S(1)}, bf16[8,1,32,64,128]{4,3,2,1,0:T(8,128)(2,1)S(1)}, bf16[8,1,32,64,128]{4,3,2,1,0:T(8,128)(2,1)S(1)}, bf16[8,1,32,64,128]{4,3,2,1,0:T(8,128)(2,1)S(1)}) fusion(f32[8,32,128]{2,1,0:T(8,128)S(1)} %gather_fusion.2, f32[8,32,128]{2,1,0:T(8,128)S(1)} %gather_fusion.3, ...), kind=kLoop, calls=%fused_computation.36.clone.1 | loop fusion | flops 37748736 | bytes 17302048 | tf_op jit(solution)/shard_map/convert
  539.6 6.1 pad_maximum_fusion.3
  545.7 8.3 fusion.88
  555.1 5.0 compare_convert_fusion.2
  572.2 63.0 %fusion.87 = (bf16[8,1,32,64,128]{4,3,2,1,0:T(8,128)(2,1)S(1)}, bf16[8,1,32,64,128]{4,3,2,1,0:T(8,128)(2,1)S(1)}, bf16[8,1,32,64,128]{4,3,2,1,0:T(8,128)(2,1)S(1)}, bf16[8,1,32,64,128]{4,3,2,1,0:T(8,128)(2,1)S(1)}) fusion(f32[8,32,128]{2,1,0:T(8,128)S(1)} %gather_fusion.2, f32[8,32,128]{2,1,0:T(8,128)S(1)} %gather_fusion.3, ...), kind=kLoop, calls=%fused_computation.36.clone.1 | loop fusion | flops 37748736 | bytes 17302048 | tf_op jit(solution)/shard_map/convert
  635.2 6.1 pad_maximum_fusion.3
  641.3 8.3 fusion.88
  650.7 5.0 compare_convert_fusion.2
  667.8 63.0 %fusion.87 = (bf16[8,1,32,64,128]{4,3,2,1,0:T(8,128)(2,1)S(1)}, bf16[8,1,32,64,128]{4,3,2,1,0:T(8,128)(2,1)S(1)}, bf16[8,1,32,64,128]{4,3,2,1,0:T(8,128)(2,1)S(1)}, bf16[8,1,32,64,128]{4,3,2,1,0:T(8,128)(2,1)S(1)}) fusion(f32[8,32,128]{2,1,0:T(8,128)S(1)} %gather_fusion.2, f32[8,32,128]{2,1,0:T(8,128)S(1)} %gather_fusion.3, ...), kind=kLoop, calls=%fused_computation.36.clone.1 | loop fusion | flops 37748736 | bytes 17302048 | tf_op jit(solution)/shard_map/convert
  730.7 6.1 pad_maximum_fusion.3
  736.8 8.3 fusion.88
  746.2 5.0 compare_convert_fusion.2
  763.3 63.0 %fusion.87 = (bf16[8,1,32,64,128]{4,3,2,1,0:T(8,128)(2,1)S(1)}, bf16[8,1,32,64,128]{4,3,2,1,0:T(8,128)(2,1)S(1)}, bf16[8,1,32,64,128]{4,3,2,1,0:T(8,128)(2,1)S(1)}, bf16[8,1,32,64,128]{4,3,2,1,0:T(8,128)(2,1)S(1)}) fusion(f32[8,32,128]{2,1,0:T(8,128)S(1)} %gather_fusion.2, f32[8,32,128]{2,1,0:T(8,128)S(1)} %gather_fusion.3, ...), kind=kLoop, calls=%fused_computation.36.clone.1 | loop fusion | flops 37748736 | bytes 17302048 | tf_op jit(solution)/shard_map/convert
  826.3 6.1 pad_maximum_fusion.3
  832.4 8.3 fusion.88
  841.8 5.0 compare_convert_fusion.2
  858.9 63.0 %fusion.87 = (bf16[8,1,32,64,128]{4,3,2,1,0:T(8,128)(2,1)S(1)}, bf16[8,1,32,64,128]{4,3,2,1,0:T(8,128)(2,1)S(1)}, bf16[8,1,32,64,128]{4,3,2,1,0:T(8,128)(2,1)S(1)}, bf16[8,1,32,64,128]{4,3,2,1,0:T(8,128)(2,1)S(1)}) fusion(f32[8,32,128]{2,1,0:T(8,128)S(1)} %gather_fusion.2, f32[8,32,128]{2,1,0:T(8,128)S(1)} %gather_fusion.3, ...), kind=kLoop, calls=%fused_computation.36.clone.1 | loop fusion | flops 37748736 | bytes 17302048 | tf_op jit(solution)/shard_map/convert
  921.8 6.1 pad_maximum_fusion.3
  927.9 8.3 fusion.88
  937.3 5.0 compare_convert_fusion.2
  954.4 63.0 %fusion.87 = (bf16[8,1,32,64,128]{4,3,2,1,0:T(8,128)(2,1)S(1)}, bf16[8,1,32,64,128]{4,3,2,1,0:T(8,128)(2,1)S(1)}, bf16[8,1,32,64,128]{4,3,2,1,0:T(8,128)(2,1)S(1)}, bf16[8,1,32,64,128]{4,3,2,1,0:T(8,128)(2,1)S(1)}) fusion(f32[8,32,128]{2,1,0:T(8,128)S(1)} %gather_fusion.2, f32[8,32,128]{2,1,0:T(8,128)S(1)} %gather_fusion.3, ...), kind=kLoop, calls=%fused_computation.36.clone.1 | loop fusion | flops 37748736 | bytes 17302048 | tf_op jit(solution)/shard_map/convert
  1017.4 6.1 pad_maximum_fusion.3
  1023.5 8.3 fusion.88
  1032.9 5.0 compare_convert_fusion.2
  1050.0 63.0 %fusion.87 = (bf16[8,1,32,64,128]{4,3,2,1,0:T(8,128)(2,1)S(1)}, bf16[8,1,32,64,128]{4,3,2,1,0:T(8,128)(2,1)S(1)}, bf16[8,1,32,64,128]{4,3,2,1,0:T(8,128)(2,1)S(1)}, bf16[8,1,32,64,128]{4,3,2,1,0:T(8,128)(2,1)S(1)}) fusion(f32[8,32,128]{2,1,0:T(8,128)S(1)} %gather_fusion.2, f32[8,32,128]{2,1,0:T(8,128)S(1)} %gather_fusion.3, ...), kind=kLoop, calls=%fused_computation.36.clone.1 | loop fusion | flops 37748736 | bytes 17302048 | tf_op jit(solution)/shard_map/convert
  1112.9 6.1 pad_maximum_fusion.3
  1119.0 8.3 fusion.88
  1128.4 5.0 compare_convert_fusion.2
  1145.5 63.0 %fusion.87 = (bf16[8,1,32,64,128]{4,3,2,1,0:T(8,128)(2,1)S(1)}, bf16[8,1,32,64,128]{4,3,2,1,0:T(8,128)(2,1)S(1)}, bf16[8,1,32,64,128]{4,3,2,1,0:T(8,128)(2,1)S(1)}, bf16[8,1,32,64,128]{4,3,2,1,0:T(8,128)(2,1)S(1)}) fusion(f32[8,32,128]{2,1,0:T(8,128)S(1)} %gather_fusion.2, f32[8,32,128]{2,1,0:T(8,128)S(1)} %gather_fusion.3, ...), kind=kLoop, calls=%fused_computation.36.clone.1 | loop fusion | flops 37748736 | bytes 17302048 | tf_op jit(solution)/shard_map/convert
  1208.5 6.1 pad_maximum_fusion.3
  1214.6 8.3 fusion.88
  1228.3 30.0 %reduce-scatter.2.cloned.1.call-done = f32[1,8,128,128]{3,2,1,0:T(8,128)} async-done(((f32[4,8,128,128]{3,2,1,0:T(8,128)}), f32[1,8,128,128]{3,2,1,0:T(8,128)}) %reduce-scatter.2.cloned.1.call-update) | async-done | bytes 524304 | tf_op jit(solution)/shard_map/reduce_scatter | solution.py:143
  1258.3 5.5 all-to-all-start
  1263.9 4.8 gather_fusion.9
  1269.7 4.8 gather_fusion.10
  1274.7 3.6 all-to-all-done
  (305 shorter events, 158.6 us)
Async XLA Ops:
  6.5 1.8 copy-start
  6.5 1251.8 %reduce-scatter.2.cloned.1.call-start = ((), (), s32[]{:S(2)}) async-start(), calls=%async_computation.2 | async-start | bytes 2621440 | tf_op jit(solution)/shard_map/reduce_scatter | solution.py:143
  63.3 1162.3 %copy-start.3 = (s32[64,12]{0,1:T(8,128)S(1)}, s32[64,12]{0,1:T(8,128)}, u32[]{:S(2)}) copy-start(s32[64,12]{0,1:T(8,128)} %param.20) | copy-start | bytes 9220
  63.3 1162.4 %copy-start.1 = (s32[128]{0:T(128)S(1)}, s32[128]{0:T(128)}, u32[]{:S(2)}) copy-start(s32[128]{0:T(128)} %param.21) | copy-start | bytes 1540
  1224.2 1.4 copy-start.2
  1258.3 20.0 %all-to-all-start = ((f32[8,128,128]{2,1,0:T(8,128)}), f32[8,128,128]{2,1,0:T(8,128)S(1)}, u32[]{:S(2)}, u32[]{:S(2)}) async-start(f32[8,128,128]{2,1,0:T(8,128)} %bitcast.98), calls=%async_computation.1 | async-start | bytes 1048576 | tf_op jit(solution)/shard_map/all_to_all | solution.py:149
Sparse Core Ops, SparseCore 0:
  1225.7 32.5 reduce-scatter.1
where the time goes:
time: 1300 us; the launch traced here: 1290 us
  other arithmetic  905 us (70%)
  local copies, waits for them, and re-layouts  165 us (13%)
  matrix products  115 us (9%)
  waiting for transfers between devices  33.6 us (3%)
  blocking collectives  33.2 us (3%)
  loops' own time  15.9 us (1%)
  between operations  13.8 us (1%)
    another operation x12, other arithmetic  755 us
    dot_general x12, matrix products, one_block(): jnp.einsum('brz,brx->bzx', depth_factor, lateral_factor, preferred_elemen...  100 us
    another operation x12, other arithmetic, pair_factors(): jnp.stack([part_real, -part_imag], axis=1).astype(jnp.bfloat16)  73.2 us
    convert_element_type x12, other arithmetic, body(): alive_flag = (slot_local < foot_count[0][centre_local]).astype(jnp.int32)  59.7 us
    all_gather x1, blocking collectives, body(): all_rows = lax.all_gather(trace_rows, 'beam', axis=0, tiled=True)  33.2 us
    gather x12, local copies, waits for them, and re-layouts, one_block(): depth_table[rows_now]  32.9 us
    gather x12, local copies, waits for them, and re-layouts, one_block(): ray_spread[rows_now]  32.9 us
    gather x12, local copies, waits for them, and re-layouts, one_block(): ray_lateral[rows_now]  32.9 us
  transfers between devices with their start and end apart: 2, of which 2 were waited for; matrix products, arithmetic and copies ran while one was open for 1% of the time, Pallas kernels for 0%

commit v1 on v0

v1 whole, which is shorter than its diff:
```python
import math

import jax
import jax.numpy as jnp
import numpy as np
from jax import lax
from jax.experimental import pallas as pl
from jax.experimental.pallas import tpu as pltpu
from jax.sharding import PartitionSpec as P

FREQUENCIES = 64
DIRECTIONS = 32
WINDOW = 32
LANES = 128
FIRST_HZ = 4.0
STEP_HZ = 60.0 / FREQUENCIES
SPANS = LANES // DIRECTIONS
STEPS = FREQUENCIES // SPANS
PARTS = 2
BLOCK = PARTS * LANES
CHUNKS = 8
CHUNK_STEPS = STEPS // CHUNKS
ROWS = 16


def fit_half_turn():
    nodes = 0.5 * np.cos((np.arange(400) + 0.5) * np.pi / 800)
    u = nodes * nodes
    sine = np.polynomial.polynomial.polyfit(u, np.sin(np.pi * nodes) / nodes, 5)
    cosine = np.polynomial.polynomial.polyfit(u, np.cos(np.pi * nodes), 6)
    return [float(v) for v in sine], [float(v) for v in cosine]


SINE, COSINE = fit_half_turn()


def horner(coefficients, u):
    total = coefficients[-1]
    for value in coefficients[-2::-1]:
        total = total * u + value
    return total


def turn(t):
    r = t - jnp.floor(t + 0.5)
    u = r * r
    s = r * horner(SINE, u)
    c = horner(COSINE, u)
    return 1.0 - 2.0 * (s * s), 2.0 * (s * c)


def stack_tables():
    freq = np.arange(FREQUENCIES, dtype=np.float32)
    angular = (2.0 * math.pi * (4.0 + 60.0 * freq / FREQUENCIES)).astype(np.float32)
    centred = (np.arange(WINDOW) - 0.5 * (WINDOW - 1)).astype(np.float32)
    taper = (np.exp(-((centred / (0.25 * WINDOW)) ** 2)) / math.sqrt(WINDOW)).astype(np.float32)
    slowness = (2e-05 * (np.arange(DIRECTIONS) - 0.5 * (DIRECTIONS - 1))).astype(np.float32)
    angle = angular[:, None, None] * slowness[None, :, None] * (25.0 * centred)[None, None, :]
    angle = angle.astype(np.float32)
    real = (taper * np.cos(angle)).astype(jnp.bfloat16).astype(np.float32)
    imag = (-taper * np.sin(angle)).astype(jnp.bfloat16).astype(np.float32)

    def lay(table):
        table = table.reshape(SPANS, STEPS, DIRECTIONS, WINDOW).transpose(1, 3, 0, 2)
        return np.ascontiguousarray(table.reshape(STEPS, WINDOW, LANES))

    return lay(real), lay(imag)


def beam_kernel(win_ref, real_ref, imag_ref, out_ref):
    centres = out_ref.shape[0]
    scale = 1.0 / math.sqrt(DIRECTIONS * FREQUENCIES)
    row = lax.broadcasted_iota(jnp.int32, (PARTS * FREQUENCIES, BLOCK), 0)
    col = lax.broadcasted_iota(jnp.int32, (PARTS * FREQUENCIES, BLOCK), 1)
    home = lax.div(col, LANES) * FREQUENCIES + lax.div(lax.rem(col, LANES), DIRECTIONS) * STEPS
    for step in range(STEPS):
        pick = jnp.where(row == home + step, 1.0, 0.0).astype(jnp.bfloat16)
        spread = jnp.dot(win_ref[...], pick, preferred_element_type=jnp.float32)
        real = jnp.zeros((centres, LANES), jnp.float32)
        imag = jnp.zeros((centres, LANES), jnp.float32)
        for k in range(WINDOW):
            tr = spread[k * centres : (k + 1) * centres, :LANES]
            ti = spread[k * centres : (k + 1) * centres, LANES:]
            sr = real_ref[step, k : k + 1, :]
            si = imag_ref[step, k : k + 1, :]
            real = real + (sr * tr - si * ti)
            imag = imag + (sr * ti + si * tr)
        out_ref[:, 2 * step, :] = real * scale
        out_ref[:, 2 * step + 1, :] = imag * scale


def beams(windows, centres):
    real, imag = stack_tables()
    return pl.pallas_call(
        beam_kernel,
        out_shape=jax.ShapeDtypeStruct((centres, PARTS * STEPS, LANES), jnp.float32),
        name="beams",
    )(windows, real, imag)


def start_phases(times, start_ref, shot):
    c, s = turn(FIRST_HZ * times)
    step_c, step_s = turn(STEP_HZ * times)
    span_c, span_s = turn((STEP_HZ * STEPS) * times)
    cs, ss = [c], [s]
    for _ in range(SPANS - 1):
        c, s = c * span_c - s * span_s, c * span_s + s * span_c
        cs.append(c)
        ss.append(s)
    start_ref[shot, 0] = jnp.concatenate(cs, axis=0).T
    start_ref[shot, 1] = jnp.concatenate(ss, axis=0).T
    start_ref[shot, 2] = jnp.concatenate([step_c] * SPANS, axis=0).T
    start_ref[shot, 3] = jnp.concatenate([step_s] * SPANS, axis=0).T


def start_lateral(lateral, spread, side_ref):
    def factor(hz):
        damping = jnp.exp((-2.0 * math.pi * hz) * spread)
        c, s = turn(hz * lateral)
        return damping * c, -(damping * s)

    re, im = factor(FIRST_HZ)
    side_ref[SPANS, 0], side_ref[SPANS, 1] = factor(STEP_HZ)
    span_re, span_im = factor(STEP_HZ * STEPS)
    for span in range(SPANS):
        side_ref[span, 0], side_ref[span, 1] = re, im
        re, im = re * span_re - im * span_im, re * span_im + im * span_re


def depth_chunk(chunk, centre, beam_ref, start_ref, state_ref, factor_ref):
    cells = start_ref.shape[2]
    for block in range(cells // ROWS):
        rows = pl.ds(block * ROWS, ROWS)
        state = []
        for shot in range(2):
            if chunk == 0:
                c0 = start_ref[shot, 0, rows, :]
                s0 = start_ref[shot, 1, rows, :]
                sc = start_ref[shot, 2, rows, :]
                ss = start_ref[shot, 3, rows, :]
                c1, s1 = c0 * sc - s0 * ss, s0 * sc + c0 * ss
                twice = 2.0 * sc
                state_ref[shot, 4, rows, :] = twice
            else:
                c0, s0, c1, s1, twice = [state_ref[shot, n, rows, :] for n in range(5)]
            state.append((c0, s0, c1, s1, twice))
        for inner in range(CHUNK_STEPS):
            step = chunk * CHUNK_STEPS + inner
            re = im = None
            for shot in range(2):
                c0, s0, c1, s1, twice = state[shot]
                br = beam_ref[shot, centre, 2 * step : 2 * step + 1, :]
                bi = beam_ref[shot, centre, 2 * step + 1 : 2 * step + 2, :]
                part_re = br * c0 - bi * s0
                part_im = br * s0 + bi * c0
                re = part_re if re is None else re + part_re
                im = part_im if im is None else im + part_im
                state[shot] = (c1, s1, twice * c1 - c0, twice * s1 - s0, twice)
            col = inner * BLOCK
            factor_ref[rows, col : col + LANES] = re.astype(jnp.bfloat16)
            factor_ref[rows, col + LANES : col + BLOCK] = im.astype(jnp.bfloat16)
        if chunk + 1 < CHUNKS:
            for shot in range(2):
                for n in range(4):
                    state_ref[shot, n, rows, :] = state[shot][n]


def lateral_chunk(chunk, side_ref, chain_ref, factor_ref):
    source = side_ref if chunk == 0 else chain_ref
    step_re, step_im = side_ref[SPANS, 0], side_ref[SPANS, 1]
    if chunk == 0:
        chain_ref[SPANS, 0], chain_ref[SPANS, 1] = step_re, step_im
    else:
        step_re, step_im = chain_ref[SPANS, 0], chain_ref[SPANS, 1]
    for span in range(SPANS):
        re, im = source[span, 0], source[span, 1]
        for inner in range(CHUNK_STEPS):
            at = inner * BLOCK + span * DIRECTIONS
            factor_ref[at : at + DIRECTIONS, :] = re.astype(jnp.bfloat16)
            factor_ref[at + LANES : at + LANES + DIRECTIONS, :] = im.astype(jnp.bfloat16)
            if chunk * CHUNK_STEPS + inner + 1 < STEPS:
                re, im = re * step_re - im * step_im, re * step_im + im * step_re
        if chunk + 1 < CHUNKS:
            chain_ref[span, 0], chain_ref[span, 1] = re, im


def one_entry(
    centre, tile, next_ref, beam_ref, out_ref, start_ref, state_ref, side_ref, chain_ref,
    depth_factors, lateral_factors,
):
    total = None
    for chunk in range(CHUNKS):
        depth_ref, lateral_ref = depth_factors[chunk % 2], lateral_factors[chunk % 2]
        depth_chunk(chunk, centre, beam_ref, start_ref, state_ref, depth_ref)
        lateral_chunk(chunk, side_ref, chain_ref, lateral_ref)
        if chunk < 2:
            start_phases(next_ref[chunk], start_ref, chunk)
        if chunk == 2:
            start_lateral(next_ref[2], next_ref[3], side_ref)
        part = jnp.dot(depth_ref[...], lateral_ref[...], preferred_element_type=jnp.float32)
        total = part if total is None else total + part
    out_ref[tile] = out_ref[tile] + total


def tile_kernel(
    meta_ref, rows_ref, centre_ref, tile_ref, beam_ref, own_ref, other_ref, lateral_ref, spread_ref,
    out_ref, start_ref, state_ref, side_ref, chain_ref, depth_even, depth_odd, lateral_even,
    lateral_odd, times_ref, sems,
):
    base, count = meta_ref[0], meta_ref[1]

    def times(n, slot):
        row = rows_ref[base + n]
        return [
            pltpu.make_async_copy(table.at[row], times_ref.at[slot, kind], sems.at[slot, kind])
            for kind, table in enumerate((own_ref, other_ref, lateral_ref, spread_ref))
        ]

    def fetch(n, slot):
        @pl.when(n < count)
        def _():
            for copy in times(n, slot):
                copy.start()

    def arrive(n, slot):
        @pl.when(n < count)
        def _():
            for copy in times(n, slot):
                copy.wait()

    fetch(0, 0)
    fetch(1, 1)
    out_ref[...] = jnp.zeros_like(out_ref)
    arrive(0, 0)

    @pl.when(count > 0)
    def _():
        for shot in range(2):
            start_phases(times_ref[0, shot], start_ref, shot)
        start_lateral(times_ref[0, 2], times_ref[0, 3], side_ref)

    def entry(n, carry):
        slot = lax.rem(n, 2)
        fetch(n + 2, slot)
        arrive(n + 1, 1 - slot)
        one_entry(
            centre_ref[base + n], tile_ref[base + n], times_ref.at[1 - slot], beam_ref, out_ref,
            start_ref, state_ref, side_ref, chain_ref, (depth_even, depth_odd),
            (lateral_even, lateral_odd),
        )
        return carry

    lax.fori_loop(0, count, entry, 0)


def tiles_of(meta, rows, centres, places, beam, depth, other_depth, lateral, spread, tile_count):
    cells, across = depth.shape[2], lateral.shape[2]
    scalars = pl.BlockSpec(memory_space=pltpu.SMEM)
    inside = pl.BlockSpec(memory_space=pltpu.VMEM)
    outside = pl.BlockSpec(memory_space=pl.ANY)
    return pl.pallas_call(
        tile_kernel,
        in_specs=[scalars] * 4 + [inside] + [outside] * 4,
        out_specs=inside,
        scratch_shapes=[
            pltpu.VMEM((2, 4, cells, LANES), jnp.float32),
            pltpu.VMEM((2, 5, cells, LANES), jnp.float32),
            pltpu.VMEM((SPANS + 1, 2, DIRECTIONS, across), jnp.float32),
            pltpu.VMEM((SPANS + 1, 2, DIRECTIONS, across), jnp.float32),
            pltpu.VMEM((cells, CHUNK_STEPS * BLOCK), jnp.bfloat16),
            pltpu.VMEM((cells, CHUNK_STEPS * BLOCK), jnp.bfloat16),
            pltpu.VMEM((CHUNK_STEPS * BLOCK, across), jnp.bfloat16),
            pltpu.VMEM((CHUNK_STEPS * BLOCK, across), jnp.bfloat16),
            pltpu.VMEM((2, 4) + depth.shape[1:], jnp.float32),
            pltpu.SemaphoreType.DMA((2, 4)),
        ],
        out_shape=jax.ShapeDtypeStruct((tile_count, cells, across), jnp.float32),
        compiler_params=pltpu.CompilerParams(vmem_limit_bytes=40 << 20),
        name="tiles_of",
    )(meta, rows, centres, places, beam, depth, other_depth, lateral, spread)


def body(
    traces, send_table, window_slots, ray_depth, ray_lateral, ray_spread,
    ray_index, foot_count, foot_tiles, tile_owner,
):
    groups = lax.axis_size("beam")
    shots = lax.axis_size("shot")
    pairs = shots // 2
    group_id = lax.axis_index("beam")
    shot_id = lax.axis_index("shot")
    pair_id, side = shot_id // 2, shot_id % 2
    swap = [(n, n ^ 1) for n in range(shots)]
    i32 = jnp.int32

    own_depth = ray_depth[0]
    other_depth = lax.ppermute(own_depth, "shot", swap)

    my_routes = lax.dynamic_index_in_dim(send_table[0], group_id, 0, keepdims=False)
    sent = traces[0][my_routes]
    arrived = lax.all_to_all(sent, "beam", split_axis=0, concat_axis=0, tiled=True)
    arrived = arrived.reshape(-1, arrived.shape[-1])
    slot_table = window_slots[0]
    centre_count = slot_table.shape[0]
    windows = arrived[slot_table.T.reshape(-1)]
    beam = beams(windows, centre_count)
    beam = jnp.stack([beam, lax.ppermute(beam, "shot", swap)])

    foot_slots = ray_index.shape[1]
    entries = centre_count * foot_slots
    slots = (entries + 1) // 2
    ids = jnp.arange(entries, dtype=i32)
    live = (jnp.arange(foot_slots, dtype=i32)[None, :] < foot_count[0][:, None]).reshape(-1)
    my_tiles = lax.dynamic_slice_in_dim(
        foot_tiles, group_id * centre_count, centre_count, 0
    ).reshape(-1)
    owner = tile_owner[my_tiles]
    owner_shot, owner_group = owner // groups, owner % groups
    phase = (pair_id - owner_shot // 2 + pairs - 1) % pairs
    key = jnp.where(live, phase * entries + ids, pairs * entries)
    place = jnp.sum((key[None, :] < key[:, None]).astype(i32), axis=1)
    row = ray_index.reshape(-1)
    tile = ((owner_shot % 2) ^ side) * groups + owner_group
    numbers = jnp.stack([row, ids // foot_slots, tile])

    def listed(which):
        wanted = 2 * jnp.arange(slots, dtype=i32) + which
        chosen = live[None, :] & (place[None, :] == wanted[:, None])
        return jnp.sum(jnp.where(chosen[None], numbers[:, None, :], 0), axis=2)

    rows, centres, places = listed(side)
    ends = jnp.sum(
        (live[None, :] & (phase[None, :] <= jnp.arange(pairs, dtype=i32)[:, None])).astype(i32),
        axis=1,
    )
    ends = (ends - side + 1) // 2
    starts = jnp.concatenate([jnp.zeros((1,), i32), ends[:-1]])


    image = None
    for n in range(pairs):
        meta = jnp.stack([starts[n], ends[n] - starts[n]])
        part = tiles_of(
            meta, rows, centres, places, beam, own_depth, other_depth, ray_lateral, ray_spread,
            2 * groups,
        )
        part = part[:groups] + lax.ppermute(part[groups:], "shot", swap)
        if n + 1 < pairs:
            part = lax.ppermute(
                part,
                "shot",
                [(2 * q + c, 2 * ((q - n - 1) % pairs) + c) for q in range(pairs) for c in range(2)],
            )
        image = part if image is None else image + part
    received = lax.all_to_all(image, "beam", split_axis=0, concat_axis=0, tiled=True)

    tile_count = tile_owner.shape[0]
    tiles_each = tile_count // (shots * groups)
    numbers = jnp.arange(tile_count, dtype=i32)
    mine = tile_owner == shot_id * groups + group_id
    rank = jnp.sum((mine[None, :] & (numbers[None, :] < numbers[:, None])).astype(i32), axis=1)
    named = jnp.any(
        foot_tiles.reshape(groups, -1, 1) == numbers[None, None, :], axis=1
    )
    slot = jnp.sum(jnp.where(named & mine[None, :], rank[None, :], 0), axis=1)
    chosen = slot[None, :] == jnp.arange(tiles_each, dtype=i32)[:, None]
    return jnp.sum(jnp.where(chosen[:, :, None, None], received[None], 0.0), axis=1)


def solution(mesh):
    in_specs = (
        P("shot", "beam", None),
        P("shot", None, None, None),
        P("shot", "beam", None),
        P("shot", "beam", None, None),
        P("beam", None, None),
        P("beam", None, None),
        P("beam", None),
        P("beam", None),
        P(),
        P(),
    )
    out_specs = P(("shot", "beam"), None, None)
    return jax.shard_map(body, mesh=mesh, in_specs=in_specs, out_specs=out_specs, check_vma=False)
```

time: 1300 us -> 135 us (0.10)
  other arithmetic: 905 us -> 6.62 us
  local copies, waits for them, and re-layouts: 165 us -> 14.7 us
  matrix products: 115 us -> 0 us
  Pallas kernels: 0 us -> 68.3 us
  blocking collectives: 33.2 us -> 0 us
  loops' own time: 15.9 us -> 0 us
    another operation x24 -> x4, other arithmetic: 829 us -> 2.29 us  [the longest x2 1.36 us: body(): meta = jnp.stack([starts[n], ends[n] - starts[n]])]
    gather x114 -> x3, local copies, waits for them, and re-layouts: 158 us -> 4.53 us  [the longest x1 1.59 us: body(): owner = tile_owner[my_tiles]]
    dot_general x17 -> x0, matrix products: 115 us -> none  [the longest x12 100 us: one_block(): jnp.einsum('brz,brx->bzx', depth_factor, lateral_factor, preferred_elemen...]
    pallas_call x0 -> x3, Pallas kernels: none -> 68.3 us  [the longest x2 65.6 us: tiles_of(): pl.pallas_call(tile_kernel, in_specs=[scalars] * 4 + [inside] + [outside]...]
    convert_element_type x12 -> x0, other arithmetic: 59.7 us -> none  [body(): alive_flag = (slot_local < foot_count[0][centre_local]).astype(jnp.int32)]
    all_gather x1 -> x0, blocking collectives: 33.2 us -> none  [body(): all_rows = lax.all_gather(trace_rows, 'beam', axis=0, tiled=True)]
    reduce_scatter x1 -> x0, waiting for transfers between devices: 30 us -> none  [body(): lax.psum_scatter(buffer.reshape(shot_count, groups, depth_cells, lateral_...]
    another operation x1 -> x0, loops' own time: 15.9 us -> none  [body(): buffer, _ = lax.scan(one_block, buffer_start, entry_ids.reshape(-1, 8))]
  transfers between devices with their start and end apart: 2 -> 7, of which waited for: 2 -> 4; matrix products, arithmetic and copies ran while one was open for 1% -> 10% of each run, Pallas kernels for 0% -> 28%
where the time goes in v1:
time: 135 us; the launch traced here: 134 us
  Pallas kernels  68.3 us (51%)
  waiting for transfers between devices  27.3 us (20%)
  starting transfers between devices  15.7 us (12%)
  local copies, waits for them, and re-layouts  14.7 us (11%)
  other arithmetic  6.62 us (5%)
  between operations  1.42 us (1%)
    pallas_call x2, Pallas kernels, tiles_of(): pl.pallas_call(tile_kernel, in_specs=[scalars] * 4 + [inside] + [outside]...  65.6 us
    all_to_all x1, waiting for transfers between devices, body(): lax.all_to_all(image, 'beam', split_axis=0, concat_axis=0, tiled=True)  13.3 us
    ppermute x1, waiting for transfers between devices, body(): lax.ppermute(part, 'shot', [(2 * q + c, 2 * ((q - n - 1) % pairs) + c) fo...  12.6 us
    all_to_all x1, starting transfers between devices, body(): lax.all_to_all(sent, 'beam', split_axis=0, concat_axis=0, tiled=True)  6.88 us
    unnamed x15, local copies, waits for them, and re-layouts  6.67 us
    all_to_all x1, starting transfers between devices, body(): lax.all_to_all(image, 'beam', split_axis=0, concat_axis=0, tiled=True)  6.12 us
    pallas_call x1, Pallas kernels, beams(): pl.pallas_call(beam_kernel, out_shape=jax.ShapeDtypeStruct((centres, PART...  2.71 us
  transfers between devices with their start and end apart: 7, of which 4 were waited for; matrix products, arithmetic and copies ran while one was open for 10% of the time, Pallas kernels for 28%

profile of v1, /device:TPU:0, one launch (start us, length us, event | category | flops | bytes accessed | tf_op | source)
XLA Modules:
  0.0 134.0 jit_solution(16984784528400887943)
XLA Ops:
  0.0 0.0 copy-start
  0.0 0.5 collective-permute-start.1
  0.5 0.7 compare_select_fusion
  1.1 0.1 reshape.448
  1.2 0.0 copy-done
  1.2 1.5 %gather_fusion.1 = bf16[256,128]{1,0:T(8,128)(2,1)} fusion(bf16[256,128]{1,0:T(8,128)(2,1)S(1)} %bitcast.36, s32[1024]{0:T(1024)S(1)} %pad_clamp_fusion.1), kind=kCustom, calls=%fused_computation.1 | custom fusion | bytes 132096 | tf_op jit(solution)/shard_map/gather | solution.py:300
  2.7 6.9 %all-to-all-start = ((bf16[8,32,128]{2,1,0:T(8,128)(2,1)}), bf16[8,32,128]{2,1,0:T(8,128)(2,1)S(1)}, u32[]{:S(2)}, u32[]{:S(2)}) async-start(bf16[8,32,128]{2,1,0:T(8,128)(2,1)} %bitcast.8), calls=%async_computation | async-start | bytes 131072 | tf_op jit(solution)/shard_map/all_to_all | solution.py:301
  9.6 0.8 stack_reshape.3
  10.4 0.7 iota_compare_fusion.2
  11.1 0.1 lt.129
  11.2 0.8 constant_dynamic-slice_fusion
  11.9 0.1 copy.18
  12.0 0.1 reshape.435
  12.1 0.8 copy.19
  12.9 0.1 reshape.437
  13.0 1.6 %gather_fusion = s32[96]{0:T(128)S(1)} fusion(s32[128]{0:T(128)} %param.21, s32[1024]{0:T(1024)S(1)} %pad_clamp_fusion.2), kind=kCustom, calls=%fused_computation | custom fusion | bytes 1152 | tf_op jit(solution)/shard_map/gather | solution.py:317
  14.7 0.1 fusion.3
  14.8 0.2 convert_reduce_fusion.1
  15.0 0.1 compare_and_fusion
  15.1 0.1 select_reduce_fusion.1
  15.3 1.2 all-to-all-done
  16.5 1.5 %gather_fusion.2 = bf16[256,128]{1,0:T(8,128)(2,1)} fusion(bf16[256,128]{1,0:T(8,128)(2,1)S(1)} %bitcast.40, s32[1024]{0:T(1024)S(1)} %pad_clamp_fusion), kind=kCustom, calls=%fused_computation.2 | custom fusion | bytes 132096 | tf_op jit(solution)/shard_map/gather | solution.py:305
  18.0 2.7 %beams.1 = f32[8,32,128]{2,1,0:T(8,128)} custom-call(bf16[256,128]{1,0:T(8,128)(2,1)} %gather_fusion.2, f32[16,32,128]{2,1,0:T(8,128)} %constant.129.clone.real_ref, f32[16,32,128]{2,1,0:T(8,128)} %constant.130.clone.imag_ref), custom_call_target="tpu_custom_call" | custom-call | tf_op jit(solution)/shard_map/beams/pallas_call | solution.py:94
  20.7 0.0 collective-permute-start
  20.7 0.6 fusion.10
  21.3 0.7 pad_add_fusion.1.meta_ref
  22.0 0.3 collective-permute-done
  22.2 0.9 pad_maximum_fusion.beam_ref
  23.2 0.0 collective-permute-done.1.other_ref
  23.2 0.0 copy-start.1
  23.2 2.2 %copy-done.1 = f32[1,256,32,128]{3,2,1,0:T(8,128)S(1)} copy-done((f32[1,256,32,128]{3,2,1,0:T(8,128)S(1)}, f32[1,256,32,128]{3,2,1,0:T(8,128)}, u32[]{:S(2)}) %copy-start.1) | copy-done | bytes 4194328
  25.4 0.0 copy-start.3
  25.4 2.2 %copy-done.3 = f32[256,32,128]{2,1,0:T(8,128)S(1)} copy-done((f32[256,32,128]{2,1,0:T(8,128)S(1)}, f32[256,32,128]{2,1,0:T(8,128)}, u32[]{:S(2)}) %copy-start.3) | copy-done | bytes 4194328
  27.6 0.0 copy-start.2
  27.6 31.4 %tiles_of.2 = f32[16,128,128]{2,1,0:T(8,128)S(1)} custom-call(s32[2]{0:T(128)S(1)} %pad_add_fusion.1.meta_ref, s32[48]{0:T(128)S(1)} %get-tuple-element.9.rows_ref, s32[48]{0:T(128)S(1)} %get-tuple-element.8.centre_ref, s32[48]{0:T(128)S(1)} %get-tuple-element.7.tile_ref, f32[2,8,32,128]{3,2,1,0:T(8,128)S(1)} %pad_maximum_fusion.beam_ref, ...), custom_call_target="tpu_custom_call" | custom-call | tf_op jit(solution)/shard_map/tiles_of/pallas_call | solution.py:261
  59.0 0.3 collective-permute-start.2
  60.5 0.7 pad_add_fusion.2.meta_ref
  61.2 0.0 copy-done.2
  61.2 0.0 copy-start.4
  61.2 2.2 %copy-done.4 = f32[256,32,128]{2,1,0:T(8,128)S(1)} copy-done((f32[256,32,128]{2,1,0:T(8,128)S(1)}, f32[256,32,128]{2,1,0:T(8,128)}, u32[]{:S(2)}) %copy-start.4) | copy-done | bytes 4194328
  63.4 34.2 %tiles_of.3 = f32[16,128,128]{2,1,0:T(8,128)S(1)} custom-call(s32[2]{0:T(128)S(1)} %pad_add_fusion.2.meta_ref, s32[48]{0:T(128)S(1)} %get-tuple-element.9.rows_ref, s32[48]{0:T(128)S(1)} %get-tuple-element.8.centre_ref, s32[48]{0:T(128)S(1)} %get-tuple-element.7.tile_ref, f32[2,8,32,128]{3,2,1,0:T(8,128)S(1)} %pad_maximum_fusion.beam_ref, ...), custom_call_target="tpu_custom_call" | custom-call | tf_op jit(solution)/shard_map/tiles_of/pallas_call | solution.py:261
  97.6 0.0 copy-start.6
  97.6 0.0 copy-start.5
  97.6 0.3 collective-permute-start.4
  98.0 0.0 collective-permute-done.2
  98.0 0.1 slice_add_fusion.1
  98.1 1.6 %collective-permute-start.3 = (f32[8,128,128]{2,1,0:T(8,128)S(1)}, f32[8,128,128]{2,1,0:T(8,128)S(1)}, u32[]{:S(2)}, u32[]{:S(2)}) collective-permute-start(f32[8,128,128]{2,1,0:T(8,128)S(1)} %slice_add_fusion.1), channel_id=1, source_target_pairs={{0,16},{8,24},{16,0},{24,8},{1,17},{9,25},{17,1},{25,9},{2,18},{10... | collective-permute-start | bytes 1572872 | tf_op jit(solution)/shard_map/ppermute | solution.py:349
  99.6 0.0 collective-permute-done.4
  99.6 12.6 %collective-permute-done.3 = f32[8,128,128]{2,1,0:T(8,128)S(1)} collective-permute-done((f32[8,128,128]{2,1,0:T(8,128)S(1)}, f32[8,128,128]{2,1,0:T(8,128)S(1)}, u32[]{:S(2)}, u32[]{:S(2)}) %collective-permute-start.3) | collective-permute-done | bytes 524320 | tf_op jit(solution)/shard_map/ppermute | solution.py:349
  112.2 0.9 fusion
  113.1 6.1 %all-to-all-start.1 = ((f32[8,128,128]{2,1,0:T(8,128)}), f32[8,128,128]{2,1,0:T(8,128)S(1)}, u32[]{:S(2)}, u32[]{:S(2)}) async-start(f32[8,128,128]{2,1,0:T(8,128)} %fusion), calls=%async_computation.1 | async-start | bytes 1048576 | tf_op jit(solution)/shard_map/all_to_all | solution.py:355
  119.2 0.0 copy-done.6
  119.2 0.1 copy.17
  119.3 0.1 eq.61
  119.4 0.0 copy-done.5
  119.4 0.1 convert_reduce_fusion
  119.5 0.2 fusion.1
  119.7 0.1 select_reduce_fusion.2
  119.8 13.3 %all-to-all-done.1 = f32[8,128,128]{2,1,0:T(8,128)S(1)} async-done(((f32[8,128,128]{2,1,0:T(8,128)}), f32[8,128,128]{2,1,0:T(8,128)S(1)}, u32[]{:S(2)}, u32[]{:S(2)}) %all-to-all-start.1) | async-done | bytes 524320 | tf_op jit(solution)/shard_map/all_to_all | solution.py:355
  133.1 0.9 select_reduce_fusion
  (15 shorter events, 0.2 us)
Async XLA Ops:
  0.0 1.2 copy-start
  0.0 23.2 %collective-permute-start.1 = (f32[256,32,128]{2,1,0:T(8,128)}, f32[256,32,128]{2,1,0:T(8,128)}, u32[]{:S(2)}, u32[]{:S(2)}) collective-permute-start(f32[256,32,128]{2,1,0:T(8,128)} %bitcast.37), channel_id=1, source_target_pairs={{0,8},{8,0},{16,24},{24,16},{1,9},{9,1},{17,25},{25,17},{2,10},{10... | collective-permute-start | bytes 12582920 | tf_op jit(solution)/shard_map/ppermute | solution.py:297
  2.7 13.8 %all-to-all-start = ((bf16[8,32,128]{2,1,0:T(8,128)(2,1)}), bf16[8,32,128]{2,1,0:T(8,128)(2,1)S(1)}, u32[]{:S(2)}, u32[]{:S(2)}) async-start(bf16[8,32,128]{2,1,0:T(8,128)(2,1)} %bitcast.8), calls=%async_computation | async-start | bytes 131072 | tf_op jit(solution)/shard_map/all_to_all | solution.py:301
  20.7 1.6 %collective-permute-start = (f32[8,32,128]{2,1,0:T(8,128)}, f32[8,32,128]{2,1,0:T(8,128)S(1)}, u32[]{:S(2)}, u32[]{:S(2)}) collective-permute-start(f32[8,32,128]{2,1,0:T(8,128)} %beams.1), channel_id=1, source_target_pairs={{0,8},{8,0},{16,24},{24,16},{1,9},{9,1},{17,25},{25,17},{2,10},{10... | collective-permute-start | bytes 393224 | tf_op jit(solution)/shard_map/ppermute | solution.py:307
  23.2 2.2 %copy-start.1 = (f32[1,256,32,128]{3,2,1,0:T(8,128)S(1)}, f32[1,256,32,128]{3,2,1,0:T(8,128)}, u32[]{:S(2)}) copy-start(f32[1,256,32,128]{3,2,1,0:T(8,128)} %param.15) | copy-start | bytes 12582916
  25.4 2.2 %copy-start.3 = (f32[256,32,128]{2,1,0:T(8,128)S(1)}, f32[256,32,128]{2,1,0:T(8,128)}, u32[]{:S(2)}) copy-start(f32[256,32,128]{2,1,0:T(8,128)} %lateral_ref.3) | copy-start | bytes 12582916
  27.6 33.6 %copy-start.2 = (f32[1,256,32,128]{3,2,1,0:T(8,128)S(1)}, f32[1,256,32,128]{3,2,1,0:T(8,128)}, u32[]{:S(2)}) copy-start(f32[1,256,32,128]{3,2,1,0:T(8,128)} %param.15) | copy-start | bytes 12582916
  59.0 39.0 %collective-permute-start.2 = (f32[8,128,128]{2,1,0:T(8,128)S(1)}, f32[8,128,128]{2,1,0:T(8,128)S(1)}, u32[]{:S(2)}, u32[]{:S(2)}) collective-permute-start(f32[8,128,128]{2,1,0:T(8,128)S(1)} %slice.32), channel_id=1, source_target_pairs={{0,8},{8,0},{16,24},{24,16},{1,9},{9,1},{17,25},{25,17},{2,10},{10... | collective-permute-start | bytes 1572872 | tf_op jit(solution)/shard_map/ppermute | solution.py:347
  61.2 2.2 %copy-start.4 = (f32[256,32,128]{2,1,0:T(8,128)S(1)}, f32[256,32,128]{2,1,0:T(8,128)}, u32[]{:S(2)}) copy-start(f32[256,32,128]{2,1,0:T(8,128)} %lateral_ref.3) | copy-start | bytes 12582916
  97.6 21.6 %copy-start.6 = (s32[64,12]{0,1:T(8,128)S(1)}, s32[64,12]{0,1:T(8,128)}, u32[]{:S(2)}) copy-start(s32[64,12]{0,1:T(8,128)} %param.20) | copy-start | bytes 9220
  97.6 21.8 %copy-start.5 = (s32[128]{0:T(128)S(1)}, s32[128]{0:T(128)}, u32[]{:S(2)}) copy-start(s32[128]{0:T(128)} %param.21) | copy-start | bytes 1540
  97.6 2.0 %collective-permute-start.4 = (f32[8,128,128]{2,1,0:T(8,128)S(1)}, f32[8,128,128]{2,1,0:T(8,128)S(1)}, u32[]{:S(2)}, u32[]{:S(2)}) collective-permute-start(f32[8,128,128]{2,1,0:T(8,128)S(1)} %slice.34), channel_id=1, source_target_pairs={{0,8},{8,0},{16,24},{24,16},{1,9},{9,1},{17,25},{25,17},{2,10},{10... | collective-permute-start | bytes 1572872 | tf_op jit(solution)/shard_map/ppermute | solution.py:347
  98.1 14.1 %collective-permute-start.3 = (f32[8,128,128]{2,1,0:T(8,128)S(1)}, f32[8,128,128]{2,1,0:T(8,128)S(1)}, u32[]{:S(2)}, u32[]{:S(2)}) collective-permute-start(f32[8,128,128]{2,1,0:T(8,128)S(1)} %slice_add_fusion.1), channel_id=1, source_target_pairs={{0,16},{8,24},{16,0},{24,8},{1,17},{9,25},{17,1},{25,9},{2,18},{10... | collective-permute-start | bytes 1572872 | tf_op jit(solution)/shard_map/ppermute | solution.py:349
  113.1 20.0 %all-to-all-start.1 = ((f32[8,128,128]{2,1,0:T(8,128)}), f32[8,128,128]{2,1,0:T(8,128)S(1)}, u32[]{:S(2)}, u32[]{:S(2)}) async-start(f32[8,128,128]{2,1,0:T(8,128)} %fusion), calls=%async_computation.1 | async-start | bytes 1048576 | tf_op jit(solution)/shard_map/all_to_all | solution.py:355

commit v2 on v1

v2 whole, which is shorter than its diff:
```python
import functools
import math

import jax
import jax.numpy as jnp
import numpy as np
from jax import lax
from jax.experimental import pallas as pl
from jax.experimental.pallas import tpu as pltpu
from jax.sharding import PartitionSpec as P

FREQUENCIES = 64
DIRECTIONS = 32
WINDOW = 32
LANES = 128
FIRST_HZ = 4.0
STEP_HZ = 60.0 / FREQUENCIES
SPANS = LANES // DIRECTIONS
STEPS = FREQUENCIES // SPANS
PARTS = 2
BLOCK = PARTS * LANES
CHUNKS = 8
CHUNK_STEPS = STEPS // CHUNKS
TIE = CHUNKS - 2
ROWS = 16


LONGEST = 0.25


def fit_half_turn(reach, sine_terms, cosine_terms):
    nodes = reach * np.cos((np.arange(400) + 0.5) * np.pi / 800)
    u = nodes * nodes
    sine = np.polynomial.polynomial.polyfit(u, np.sin(np.pi * nodes) / nodes, sine_terms - 1)
    cosine = np.polynomial.polynomial.polyfit(u, np.cos(np.pi * nodes), cosine_terms - 1)
    return [float(v) for v in sine], [float(v) for v in cosine]


WIDE = fit_half_turn(0.5, 5, 5)
NARROW = fit_half_turn(STEP_HZ * LONGEST, 4, 4)


def horner(coefficients, u):
    total = coefficients[-1]
    for value in coefficients[-2::-1]:
        total = total * u + value
    return total


def half_turn(r, fits):
    u = r * r
    return horner(fits[1], u), r * horner(fits[0], u)


def first_phase(times):
    c, s = half_turn(FIRST_HZ * times - 0.5, WIDE)
    twice = s + s
    return twice * s - 1.0, -(twice * c)


def step_phase(times):
    c, s = half_turn(STEP_HZ * times, NARROW)
    twice = s + s
    return 1.0 - twice * s, twice * c


def span_phase(c, s):
    for _ in range(STEPS.bit_length() - 1):
        twice = s + s
        c, s = 1.0 - twice * s, twice * c
    return c, s


def stack_tables():
    freq = np.arange(FREQUENCIES, dtype=np.float32)
    angular = (2.0 * math.pi * (4.0 + 60.0 * freq / FREQUENCIES)).astype(np.float32)
    centred = (np.arange(WINDOW) - 0.5 * (WINDOW - 1)).astype(np.float32)
    taper = (np.exp(-((centred / (0.25 * WINDOW)) ** 2)) / math.sqrt(WINDOW)).astype(np.float32)
    slowness = (2e-05 * (np.arange(DIRECTIONS) - 0.5 * (DIRECTIONS - 1))).astype(np.float32)
    angle = angular[:, None, None] * slowness[None, :, None] * (25.0 * centred)[None, None, :]
    angle = angle.astype(np.float32)
    real = (taper * np.cos(angle)).astype(jnp.bfloat16).astype(np.float32)
    imag = (-taper * np.sin(angle)).astype(jnp.bfloat16).astype(np.float32)

    def lay(table):
        table = table.reshape(SPANS, STEPS, DIRECTIONS, WINDOW).transpose(1, 3, 0, 2)
        return np.ascontiguousarray(table.reshape(STEPS, WINDOW, LANES))

    return lay(real), lay(imag)


def pick_rows(table, held, across):
    outer, inner = table.shape
    count = outer * inner
    n = lax.broadcasted_iota(jnp.int32, (count, outer), 0)
    m = lax.broadcasted_iota(jnp.int32, (count, inner), 0)
    n, m = (lax.rem(n, outer), lax.div(m, outer)) if across else (lax.div(n, inner), lax.rem(m, inner))
    of_row = jnp.where(lax.broadcasted_iota(jnp.int32, (count, outer), 1) == n, 1.0, 0.0)
    spread = jnp.dot(
        of_row, table.astype(jnp.float32), precision=lax.Precision.HIGHEST,
        preferred_element_type=jnp.float32,
    )
    kept = jnp.where(lax.broadcasted_iota(jnp.int32, (count, inner), 1) == m, spread, 0.0)
    number = jnp.sum(kept, axis=1, keepdims=True).astype(jnp.int32)
    choice = lax.broadcasted_iota(jnp.int32, (count, held.shape[0]), 1) == number
    choice = jnp.where(choice, 1.0, 0.0).astype(jnp.bfloat16)
    return jnp.dot(choice, held, preferred_element_type=jnp.float32).astype(jnp.bfloat16)


def route_kernel(table_ref, held_ref, out_ref):
    table = table_ref[0, lax.axis_index("beam")]
    out_ref[...] = pick_rows(table, held_ref[0], False).reshape(out_ref.shape)


def routed(table, held):
    return pl.pallas_call(
        route_kernel,
        out_shape=jax.ShapeDtypeStruct(table.shape[2:] + held.shape[2:], held.dtype),
        name="routed",
    )(table, held)


def beam_kernel(slot_ref, arrived_ref, real_ref, imag_ref, out_ref):
    centres = out_ref.shape[0]
    windows = pick_rows(slot_ref[0], arrived_ref[...], True)
    scale = 1.0 / math.sqrt(DIRECTIONS * FREQUENCIES)
    row = lax.broadcasted_iota(jnp.int32, (PARTS * FREQUENCIES, BLOCK), 0)
    col = lax.broadcasted_iota(jnp.int32, (PARTS * FREQUENCIES, BLOCK), 1)
    home = lax.div(col, LANES) * FREQUENCIES + lax.div(lax.rem(col, LANES), DIRECTIONS) * STEPS
    for step in range(STEPS):
        pick = jnp.where(row == home + step, 1.0, 0.0).astype(jnp.bfloat16)
        spread = jnp.dot(windows, pick, preferred_element_type=jnp.float32)
        real = jnp.zeros((centres, LANES), jnp.float32)
        imag = jnp.zeros((centres, LANES), jnp.float32)
        for k in range(WINDOW):
            tr = spread[k * centres : (k + 1) * centres, :LANES]
            ti = spread[k * centres : (k + 1) * centres, LANES:]
            sr = real_ref[step, k : k + 1, :]
            si = imag_ref[step, k : k + 1, :]
            real = real + (sr * tr - si * ti)
            imag = imag + (sr * ti + si * tr)
        out_ref[:, 2 * step, :] = real * scale
        out_ref[:, 2 * step + 1, :] = imag * scale


def beams(slots, arrived, centres):
    real, imag = stack_tables()
    return pl.pallas_call(
        beam_kernel,
        out_shape=jax.ShapeDtypeStruct((centres, PARTS * STEPS, LANES), jnp.float32),
        name="beams",
    )(slots, arrived, real, imag)


def start_phases(times, start_ref, shot):
    c, s = first_phase(times)
    step_c, step_s = step_phase(times)
    span_c, span_s = span_phase(step_c, step_s)
    cs, ss = [c], [s]
    for _ in range(SPANS - 1):
        c, s = c * span_c - s * span_s, c * span_s + s * span_c
        cs.append(c)
        ss.append(s)
    mark = None
    for n, pieces in enumerate((cs, ss, [step_c] * SPANS, [step_s] * SPANS)):
        turned = jnp.concatenate(pieces, axis=0).T
        start_ref[shot, n] = turned
        last = turned[-ROWS:]
        mark = last if mark is None else mark + last
    return mark


def start_lateral(lateral, spread, side_ref):
    def damped(hz, phase):
        damping = jnp.exp((-2.0 * math.pi * hz) * spread)
        return damping * phase[0], -(damping * phase[1])

    re, im = damped(FIRST_HZ, first_phase(lateral))
    step_re, step_im = damped(STEP_HZ, step_phase(lateral))
    side_ref[SPANS, 0], side_ref[SPANS, 1] = step_re, step_im
    span_re, span_im = step_re, step_im
    for _ in range(STEPS.bit_length() - 1):
        span_re, span_im = span_re * span_re - span_im * span_im, 2.0 * (span_re * span_im)
    for span in range(SPANS):
        side_ref[span, 0], side_ref[span, 1] = re, im
        re, im = re * span_re - im * span_im, re * span_im + im * span_re


def depth_chunk(chunk, centre, beam_refs, start_ref, state_ref, factor_ref, marks):
    cells = start_ref.shape[2]
    for block in range(cells // ROWS):
        rows = pl.ds(block * ROWS, ROWS)
        state = []
        for shot in range(2):
            if chunk == 0:
                c0 = start_ref[shot, 0, rows, :]
                s0 = start_ref[shot, 1, rows, :]
                sc = start_ref[shot, 2, rows, :]
                ss = start_ref[shot, 3, rows, :]
                c1, s1 = c0 * sc - s0 * ss, s0 * sc + c0 * ss
                twice = 2.0 * sc
                state_ref[shot, 4, rows, :] = twice
            else:
                c0, s0, c1, s1, twice = [state_ref[shot, n, rows, :] for n in range(5)]
                if chunk == TIE and block == 0:
                    c0 = jnp.where(marks[shot] > 100.0, marks[shot], c0)
            state.append((c0, s0, c1, s1, twice))
        for inner in range(CHUNK_STEPS):
            step = chunk * CHUNK_STEPS + inner
            re = im = None
            for shot in range(2):
                c0, s0, c1, s1, twice = state[shot]
                br = beam_refs[shot][centre, 2 * step : 2 * step + 1, :]
                bi = beam_refs[shot][centre, 2 * step + 1 : 2 * step + 2, :]
                part_re = br * c0 - bi * s0
                part_im = br * s0 + bi * c0
                re = part_re if re is None else re + part_re
                im = part_im if im is None else im + part_im
                state[shot] = (c1, s1, twice * c1 - c0, twice * s1 - s0, twice)
            col = inner * BLOCK
            factor_ref[rows, col : col + LANES] = re.astype(jnp.bfloat16)
            factor_ref[rows, col + LANES : col + BLOCK] = im.astype(jnp.bfloat16)
        if chunk + 1 < CHUNKS:
            for shot in range(2):
                for n in range(4):
                    state_ref[shot, n, rows, :] = state[shot][n]


def lateral_chunk(chunk, side_ref, chain_ref, factor_ref):
    source = side_ref if chunk == 0 else chain_ref
    step_re, step_im = side_ref[SPANS, 0], side_ref[SPANS, 1]
    if chunk == 0:
        chain_ref[SPANS, 0], chain_ref[SPANS, 1] = step_re, step_im
    else:
        step_re, step_im = chain_ref[SPANS, 0], chain_ref[SPANS, 1]
    for span in range(SPANS):
        re, im = source[span, 0], source[span, 1]
        for inner in range(CHUNK_STEPS):
            at = inner * BLOCK + span * DIRECTIONS
            factor_ref[at : at + DIRECTIONS, :] = re.astype(jnp.bfloat16)
            factor_ref[at + LANES : at + LANES + DIRECTIONS, :] = im.astype(jnp.bfloat16)
            if chunk * CHUNK_STEPS + inner + 1 < STEPS:
                re, im = re * step_re - im * step_im, re * step_im + im * step_re
        if chunk + 1 < CHUNKS:
            chain_ref[span, 0], chain_ref[span, 1] = re, im


def product(chunk, depth_factors, lateral_factors):
    return jnp.dot(
        depth_factors[chunk % 2][...],
        lateral_factors[chunk % 2][...],
        preferred_element_type=jnp.float32,
    )


def one_entry(
    centre, tile, last_tile, next_ref, beam_refs, image_ref, start_ref, state_ref, side_ref,
    chain_ref, depth_factors, lateral_factors,
):
    total, marks = None, []
    for chunk in range(CHUNKS):
        part = product(chunk - 1, depth_factors, lateral_factors)
        if chunk == 0:
            image_ref[last_tile] = image_ref[last_tile] + part
        else:
            total = part if total is None else total + part
        depth_chunk(
            chunk, centre, beam_refs, start_ref, state_ref, depth_factors[chunk % 2], marks
        )
        lateral_chunk(chunk, side_ref, chain_ref, lateral_factors[chunk % 2])
        if chunk < 2:
            marks.append(start_phases(next_ref[chunk], start_ref, chunk))
        if chunk == 2:
            start_lateral(next_ref[2], next_ref[3], side_ref)
    image_ref[tile] = image_ref[tile] + total


def steps_on(entry, counts):
    centre, slot = entry
    return settle(centre, slot + 2, counts, 2)


def settle(centre, slot, counts, most):
    for _ in range(most):
        held = counts[0, jnp.minimum(centre, counts.shape[1] - 1)]
        over = slot >= held
        slot = jnp.where(over, slot - held, slot)
        centre = jnp.where(over, centre + 1, centre)
    return centre, slot


def ray_row(entry, index_ref):
    centres, slots = index_ref.shape
    return index_ref[jnp.minimum(entry[0], centres - 1), jnp.minimum(entry[1], slots - 1)]


def first_entry(counts):
    side = lax.rem(lax.axis_index("shot"), 2)
    return settle(jnp.int32(0), side, counts, 1)


def first_kernel(
    count_ref, index_ref, own_ref, other_ref, lateral_ref, spread_ref, start_ref, side_ref,
    times_ref, sems,
):
    row = ray_row(first_entry(count_ref), index_ref)
    copies = first_times(row, (own_ref, other_ref, lateral_ref, spread_ref), times_ref, sems)
    for copy in copies:
        copy.start()
    for copy in copies:
        copy.wait()
    for shot in range(2):
        start_phases(times_ref[shot], start_ref, shot)
    start_lateral(times_ref[2], times_ref[3], side_ref)


def first_times(row, tables, times_ref, sems):
    return [
        pltpu.make_async_copy(table.at[row], times_ref.at[kind], sems.at[kind])
        for kind, table in enumerate(tables)
    ]


def first_of(foot_count, ray_index, tables):
    cells, across = tables[0].shape[2], tables[2].shape[2]
    scalars = pl.BlockSpec(memory_space=pltpu.SMEM)
    inside = pl.BlockSpec(memory_space=pltpu.VMEM)
    outside = pl.BlockSpec(memory_space=pltpu.HBM)
    return pl.pallas_call(
        first_kernel,
        in_specs=[scalars] * 2 + [outside] * 4,
        out_specs=[inside, inside],
        scratch_shapes=[
            pltpu.VMEM((4,) + tables[0].shape[1:], jnp.float32),
            pltpu.SemaphoreType.DMA((4,)),
        ],
        out_shape=[
            jax.ShapeDtypeStruct((2, 4, cells, LANES), jnp.float32),
            jax.ShapeDtypeStruct((SPANS + 1, 2, DIRECTIONS, across), jnp.float32),
        ],
        name="first_of",
    )(foot_count, ray_index, *tables)


def tile_kernel(
    count_ref, index_ref, tiles_ref, owner_ref, first_start, first_side, own_beam, other_beam,
    own_ref, other_ref, lateral_ref, spread_ref, mine_ref, theirs_ref, image_ref, start_ref,
    state_ref, side_ref, chain_ref, depth_even, depth_odd, lateral_even, lateral_odd, times_ref,
    sems,
):
    group, side = lax.axis_index("beam"), lax.rem(lax.axis_index("shot"), 2)
    groups = lax.axis_size("beam")
    half = mine_ref.shape[0]
    centres = index_ref.shape[0]
    found = count_ref[0, 0]
    for n in range(1, centres):
        found = found + count_ref[0, n]
    count = lax.div(found - side + 1, 2)
    depth_factors, lateral_factors = (depth_even, depth_odd), (lateral_even, lateral_odd)
    tables = (own_ref, other_ref, lateral_ref, spread_ref)

    def times(entry, slot):
        return first_times(ray_row(entry, index_ref), tables, times_ref.at[slot], sems.at[slot])

    def fetch(entry, slot):
        for copy in times(entry, slot):
            copy.start()

    def arrive(entry, slot):
        for copy in times(entry, slot):
            copy.wait()

    def tile_of(entry):
        owner = owner_ref[tiles_ref[group * centres + entry[0], entry[1]]]
        shot, home = lax.div(owner, groups), lax.rem(owner, groups)
        away = jnp.where(lax.rem(shot, 2) == side, 0, half)
        return lax.div(shot, 2) * groups + home + away

    def one(n, carry):
        entry, later, last = carry
        slot = lax.rem(n, 2)
        after = steps_on(later, count_ref)
        arrive(later, 1 - slot)
        fetch(after, slot)
        tile = tile_of(entry)
        one_entry(
            entry[0], tile, last, times_ref.at[1 - slot], (own_beam, other_beam), image_ref,
            start_ref, state_ref, side_ref, chain_ref, depth_factors, lateral_factors,
        )
        return later, after, tile

    first = first_entry(count_ref)
    second = steps_on(first, count_ref)
    fetch(second, 1)
    image_ref[...] = jnp.zeros_like(image_ref)
    depth_odd[...] = jnp.zeros_like(depth_odd)
    lateral_odd[...] = jnp.zeros_like(lateral_odd)
    start_ref[...] = first_start[...]
    side_ref[...] = first_side[...]
    _, later, last = lax.fori_loop(0, count, one, (first, second, jnp.int32(0)))
    arrive(later, lax.rem(count + 1, 2))
    part = product(CHUNKS - 1, depth_factors, lateral_factors)
    image_ref[last] = image_ref[last] + part
    mine_ref[...] = image_ref[:half]
    theirs_ref[...] = image_ref[half:].astype(theirs_ref.dtype)


def tiles_of(entries, firsts, beams, tables, tiles):
    cells, across = tables[0].shape[2], tables[2].shape[2]
    scalars = pl.BlockSpec(memory_space=pltpu.SMEM)
    inside = pl.BlockSpec(memory_space=pltpu.VMEM)
    outside = pl.BlockSpec(memory_space=pltpu.HBM)
    return pl.pallas_call(
        tile_kernel,
        in_specs=[scalars] * 4 + [inside] * 4 + [outside] * 4,
        out_specs=[inside] * 2,
        scratch_shapes=[
            pltpu.VMEM((2 * tiles, cells, across), jnp.float32),
            pltpu.VMEM((2, 4, cells, LANES), jnp.float32),
            pltpu.VMEM((2, 5, cells, LANES), jnp.float32),
            pltpu.VMEM((SPANS + 1, 2, DIRECTIONS, across), jnp.float32),
            pltpu.VMEM((SPANS + 1, 2, DIRECTIONS, across), jnp.float32),
            pltpu.VMEM((cells, CHUNK_STEPS * BLOCK), jnp.bfloat16),
            pltpu.VMEM((cells, CHUNK_STEPS * BLOCK), jnp.bfloat16),
            pltpu.VMEM((CHUNK_STEPS * BLOCK, across), jnp.bfloat16),
            pltpu.VMEM((CHUNK_STEPS * BLOCK, across), jnp.bfloat16),
            pltpu.VMEM((2, 4) + tables[0].shape[1:], jnp.float32),
            pltpu.SemaphoreType.DMA((2, 4)),
        ],
        out_shape=[
            jax.ShapeDtypeStruct((tiles, cells, across), kind)
            for kind in (jnp.float32, jnp.bfloat16)
        ],
        compiler_params=pltpu.CompilerParams(vmem_limit_bytes=60 << 20),
        cost_estimate=pl.CostEstimate(
            flops=40_000_000_000, transcendentals=0, bytes_accessed=4_000_000
        ),
        name="tiles_of",
    )(*entries, *firsts, *beams, *tables)


def body(
    traces, send_table, window_slots, ray_depth, ray_lateral, ray_spread,
    ray_index, foot_count, foot_tiles, tile_owner,
):
    groups = lax.axis_size("beam")
    shots = lax.axis_size("shot")
    pairs = shots // 2
    group_id = lax.axis_index("beam")
    shot_id = lax.axis_index("shot")
    swap = [(n, n ^ 1) for n in range(shots)]
    i32 = jnp.int32

    own_depth = ray_depth[0]
    other_depth = lax.ppermute(own_depth, "shot", swap)

    sent = routed(send_table, traces)
    arrived = lax.all_to_all(sent, "beam", split_axis=0, concat_axis=0, tiled=True)
    arrived = arrived.reshape(-1, arrived.shape[-1])
    tables = (own_depth, other_depth, ray_lateral, ray_spread)
    firsts = first_of(foot_count, ray_index, tables)
    entries = (foot_count, ray_index, foot_tiles, tile_owner)
    arrived, firsts = lax.optimization_barrier((arrived, firsts))
    own_beam = beams(window_slots, arrived, window_slots.shape[1])
    other_beam = lax.ppermute(own_beam, "shot", swap)

    image, theirs = tiles_of(entries, firsts, (own_beam, other_beam), tables, pairs * groups)
    image = image + lax.ppermute(theirs, "shot", swap).astype(jnp.float32)
    same_side = [
        [(2 * q + c) * groups + n for q in range(pairs) for n in range(groups)] for c in range(2)
    ]
    received = lax.all_to_all(
        image.astype(jnp.bfloat16), ("shot", "beam"), split_axis=0, concat_axis=0, tiled=True,
        axis_index_groups=same_side,
    )

    tile_count = tile_owner.shape[0]
    tiles_each = tile_count // (shots * groups)
    numbers = jnp.arange(tile_count, dtype=i32)
    mine = tile_owner == shot_id * groups + group_id
    rank = jnp.sum((mine[None, :] & (numbers[None, :] < numbers[:, None])).astype(i32), axis=1)
    named = jnp.any(
        foot_tiles.reshape(groups, -1, 1) == numbers[None, None, :], axis=1
    )
    slot = jnp.sum(jnp.where(named & mine[None, :], rank[None, :], 0), axis=1)
    chosen = slot[None, :] == jnp.arange(tiles_each, dtype=i32)[:, None]
    received = received.reshape((pairs, groups) + received.shape[1:]).astype(jnp.float32)
    received = jnp.sum(received, axis=0)
    return jnp.sum(jnp.where(chosen[:, :, None, None], received[None], 0.0), axis=1)


def solution(mesh):
    in_specs = (
        P("shot", "beam", None),
        P("shot", None, None, None),
        P("shot", "beam", None),
        P("shot", "beam", None, None),
        P("beam", None, None),
        P("beam", None, None),
        P("beam", None),
        P("beam", None),
        P(),
        P(),
    )
    out_specs = P(("shot", "beam"), None, None)
    return jax.shard_map(body, mesh=mesh, in_specs=in_specs, out_specs=out_specs, check_vma=False)
```

time: 135 us -> 110 us (0.81)
  local copies, waits for them, and re-layouts: 14.7 us -> 2.05 us
  waiting for transfers between devices: 27.3 us -> 22.2 us
  starting transfers between devices: 15.7 us -> 11.1 us
  other arithmetic: 6.62 us -> 3.59 us
  Pallas kernels: 68.3 us -> 70.1 us
    ppermute x4 -> x2, waiting for transfers between devices: 12.8 us -> 2.83 us  [the longest x1 1.97 us: body(): image = image + lax.ppermute(theirs, 'shot', swap).astype(jnp.float32)]
    unnamed x15 -> x11, local copies, waits for them, and re-layouts: 6.67 us -> 1.97 us
    gather x3 -> x0, local copies, waits for them, and re-layouts: 4.53 us -> none  [the longest x1 1.59 us: body(): owner = tile_owner[my_tiles]]
    all_to_all x1, waiting for transfers between devices: 1.24 us -> 4.28 us  [body(): lax.all_to_all(sent, 'beam', split_axis=0, concat_axis=0, tiled=True)]
    all_to_all x1, starting transfers between devices: 6.12 us -> 3.57 us  [body(): lax.all_to_all(image.astype(jnp.bfloat16), ('shot', 'beam'), split_axis=0...]
    another operation x4 -> x0, other arithmetic: 2.29 us -> none  [the longest x2 1.36 us: body(): meta = jnp.stack([starts[n], ends[n] - starts[n]])]
    convert_element_type x0 -> x1, other arithmetic: none -> 2.15 us  [body(): image.astype(jnp.bfloat16)]
    ppermute x4 -> x2, starting transfers between devices: 2.2 us -> 0.22 us  [the longest x1 0.21 us: body(): image = image + lax.ppermute(theirs, 'shot', swap).astype(jnp.float32)]
  transfers between devices with their start and end apart: 7 -> 5, of which waited for: 4 -> 4; matrix products, arithmetic and copies ran while one was open for 10% -> 1% of each run, Pallas kernels for 28% -> 4%
where the time goes in v2:
time: 110 us; the launch traced here: 109 us
  Pallas kernels  70.1 us (64%)
  waiting for transfers between devices  22.2 us (20%)
  starting transfers between devices  11.1 us (10%)
  other arithmetic  3.59 us (3%)
  local copies, waits for them, and re-layouts  2.05 us (2%)
    pallas_call x1, Pallas kernels, tiles_of(): pl.pallas_call(tile_kernel, in_specs=[scalars] * 4 + [inside] * 4 + [outs...  62.3 us
    all_to_all x1, waiting for transfers between devices, body(): lax.all_to_all(image.astype(jnp.bfloat16), ('shot', 'beam'), split_axis=0...  15.1 us
    all_to_all x1, starting transfers between devices, body(): lax.all_to_all(sent, 'beam', split_axis=0, concat_axis=0, tiled=True)  6.83 us
    all_to_all x1, waiting for transfers between devices, body(): lax.all_to_all(sent, 'beam', split_axis=0, concat_axis=0, tiled=True)  4.28 us
    all_to_all x1, starting transfers between devices, body(): lax.all_to_all(image.astype(jnp.bfloat16), ('shot', 'beam'), split_axis=0...  3.57 us
    pallas_call x1, Pallas kernels, beams(): pl.pallas_call(beam_kernel, out_shape=jax.ShapeDtypeStruct((centres, PART...  3.21 us
    pallas_call x1, Pallas kernels, first_of(): pl.pallas_call(first_kernel, in_specs=[scalars] * 2 + [outside] * 4, out_...  2.61 us
  transfers between devices with their start and end apart: 5, of which 4 were waited for; matrix products, arithmetic and copies ran while one was open for 1% of the time, Pallas kernels for 4%

profile of v2, /device:TPU:0, one launch (start us, length us, event | category | flops | bytes accessed | tf_op | source)
XLA Modules:
  0.0 109.0 jit_solution(3634389967695427060)
XLA Ops:
  0.0 0.5 collective-permute-start
  0.5 2.0 %routed.1 = bf16[8,32,128]{2,1,0:T(8,128)(2,1)} custom-call(s32[1,8,8,32]{3,2,1,0:T(8,128)} %table_ref.1, bf16[1,256,128]{2,1,0:T(8,128)(2,1)} %held_ref.1), custom_call_target="tpu_custom_call" | custom-call | tf_op jit(solution)/shard_map/routed/pallas_call | solution.py:116
  2.5 6.8 %all-to-all-start = ((bf16[8,32,128]{2,1,0:T(8,128)(2,1)}), bf16[8,32,128]{2,1,0:T(8,128)(2,1)S(1)}, u32[]{:S(2)}, u32[]{:S(2)}) async-start(bf16[8,32,128]{2,1,0:T(8,128)(2,1)} %routed.1), calls=%async_computation | async-start | bytes 131072 | tf_op jit(solution)/shard_map/all_to_all | solution.py:458
  9.3 0.0 copy-start.2
  9.3 0.0 collective-permute-done.other_ref
  9.3 2.6 %first_of.1 = (f32[2,4,128,128]{3,2,1,0:T(8,128)}, f32[5,2,32,128]{3,2,1,0:T(8,128)}) custom-call(s32[1,8]{1,0:T(1,128)} %count_ref.3, s32[8,12]{1,0:T(8,128)} %index_ref.3, f32[256,32,128]{2,1,0:T(8,128)} %bitcast.5, f32[256,32,128]{2,1,0:T(8,128)} %collective-permute-done.other_ref, f32[256,32,128]{2,1,0:T(8,128)} %lateral_ref.3, f32[256,32,128]{2,1,0:T(8,128)} %spread_ref.3), custom_call_target="tpu_custom_call" | custom-call | tf_op jit(solution)/shard_map/first_of/pallas_call | solution.py:329
  11.9 4.3 %all-to-all-done = bf16[8,32,128]{2,1,0:T(8,128)(2,1)S(1)} async-done(((bf16[8,32,128]{2,1,0:T(8,128)(2,1)}), bf16[8,32,128]{2,1,0:T(8,128)(2,1)S(1)}, u32[]{:S(2)}, u32[]{:S(2)}) %all-to-all-start) | async-done | bytes 65568 | tf_op jit(solution)/shard_map/all_to_all | solution.py:458
  16.2 0.0 copy-start
  16.2 0.6 copy-done
  16.8 3.2 %beams.1.own_beam = f32[8,32,128]{2,1,0:T(8,128)} custom-call(s32[1,8,32]{2,1,0:T(8,128)} %slot_ref.1, bf16[256,128]{1,0:T(8,128)(2,1)} %bitcast.8, f32[16,32,128]{2,1,0:T(8,128)} %constant.20.clone.real_ref, f32[16,32,128]{2,1,0:T(8,128)} %constant.21.clone.imag_ref), custom_call_target="tpu_custom_call" | custom-call | tf_op jit(solution)/shard_map/beams/pallas_call | solution.py:148
  20.0 0.0 collective-permute-start.1
  20.0 0.0 copy-done.2
  20.0 0.7 copy.16.tiles_ref
  20.7 0.0 copy-start.1
  20.7 0.0 copy-start.4
  20.7 0.9 collective-permute-done.1.other_beam
  21.6 0.0 copy-start.3
  21.6 0.6 copy-done.3
  22.2 62.3 %tiles_of.1 = (f32[16,128,128]{2,1,0:T(8,128)}, bf16[16,128,128]{2,1,0:T(8,128)(2,1)}) custom-call(s32[1,8]{1,0:T(1,128)} %count_ref.3, s32[8,12]{1,0:T(8,128)} %index_ref.3, s32[64,12]{1,0:T(8,128)} %copy.16.tiles_ref, s32[128]{0:T(128)} %owner_ref.1, f32[2,4,128,128]{3,2,1,0:T(8,128)} %get-tuple-element.14.first_start, ...), custom_call_target="tpu_custom_call" | custom-call | flops 40000000000 | bytes 4000000 | tf_op jit(solution)/shard_map/tiles_of/pallas_call | solution.py:413
  84.5 0.2 collective-permute-start.2
  84.7 2.0 %collective-permute-done.2 = bf16[16,128,128]{2,1,0:T(8,128)(2,1)S(1)} collective-permute-done((bf16[16,128,128]{2,1,0:T(8,128)(2,1)}, bf16[16,128,128]{2,1,0:T(8,128)(2,1)S(1)}, u32[]{:S(2)}, u32[]{:S(2)}) %collective-permute-start.2) | collective-permute-done | bytes 524320 | tf_op jit(solution)/shard_map/ppermute | solution.py:468
  86.7 2.1 %add_convert_fusion = bf16[16,128,128]{2,1,0:T(8,128)(2,1)} fusion(f32[16,128,128]{2,1,0:T(8,128)} %get-tuple-element.17, bf16[16,128,128]{2,1,0:T(8,128)(2,1)S(1)} %collective-permute-done.2), kind=kLoop, calls=%fused_computation.2 | loop fusion | flops 786432 | bytes 2097152 | tf_op jit(solution)/shard_map/convert_element_type | solution.py:473
  88.8 3.6 %all-to-all-start.1 = ((bf16[16,128,128]{2,1,0:T(8,128)(2,1)}), bf16[16,128,128]{2,1,0:T(8,128)(2,1)S(1)}, u32[]{:S(2)}, u32[]{:S(2)}) async-start(bf16[16,128,128]{2,1,0:T(8,128)(2,1)} %add_convert_fusion), calls=%async_computation.1 | async-start | bytes 1048576 | tf_op jit(solution)/shard_map/all_to_all | solution.py:472
  92.4 0.0 copy-done.1
  92.4 0.1 eq.38
  92.5 0.0 copy-done.4
  92.5 0.1 convert_reduce_fusion.1
  92.6 0.2 fusion
  92.8 0.1 select_reduce_fusion.1
  93.0 15.1 %all-to-all-done.1 = bf16[16,128,128]{2,1,0:T(8,128)(2,1)S(1)} async-done(((bf16[16,128,128]{2,1,0:T(8,128)(2,1)}), bf16[16,128,128]{2,1,0:T(8,128)(2,1)S(1)}, u32[]{:S(2)}, u32[]{:S(2)}) %all-to-all-start.1) | async-done | bytes 524320 | tf_op jit(solution)/shard_map/all_to_all | solution.py:472
  108.0 0.1 convert_reduce_fusion
  108.1 0.9 select_reduce_fusion
  (2 shorter events, 0.0 us)
Async XLA Ops:
  0.0 9.3 %collective-permute-start = (f32[256,32,128]{2,1,0:T(8,128)}, f32[256,32,128]{2,1,0:T(8,128)}, u32[]{:S(2)}, u32[]{:S(2)}) collective-permute-start(f32[256,32,128]{2,1,0:T(8,128)} %bitcast.4), channel_id=1, source_target_pairs={{0,8},{8,0},{16,24},{24,16},{1,9},{9,1},{17,25},{25,17},{2,10},{10... | collective-permute-start | bytes 12582920 | tf_op jit(solution)/shard_map/ppermute | solution.py:455
  2.5 13.7 %all-to-all-start = ((bf16[8,32,128]{2,1,0:T(8,128)(2,1)}), bf16[8,32,128]{2,1,0:T(8,128)(2,1)S(1)}, u32[]{:S(2)}, u32[]{:S(2)}) async-start(bf16[8,32,128]{2,1,0:T(8,128)(2,1)} %routed.1), calls=%async_computation | async-start | bytes 131072 | tf_op jit(solution)/shard_map/all_to_all | solution.py:458
  9.3 10.7 %copy-start.2 = (s32[64,12]{0,1:T(8,128)S(1)}, s32[64,12]{0,1:T(8,128)}, u32[]{:S(2)}) copy-start(s32[64,12]{0,1:T(8,128)} %param.20) | copy-start | bytes 9220
  16.2 0.6 copy-start
  20.0 1.6 %collective-permute-start.1 = (f32[8,32,128]{2,1,0:T(8,128)}, f32[8,32,128]{2,1,0:T(8,128)S(1)}, u32[]{:S(2)}, u32[]{:S(2)}) collective-permute-start(f32[8,32,128]{2,1,0:T(8,128)} %beams.1.own_beam), channel_id=1, source_target_pairs={{0,8},{8,0},{16,24},{24,16},{1,9},{9,1},{17,25},{25,17},{2,10},{10... | collective-permute-start | bytes 393224 | tf_op jit(solution)/shard_map/ppermute | solution.py:465
  20.7 71.7 %copy-start.1 = (s32[64,12]{1,0:T(8,128)S(1)}, s32[64,12]{1,0:T(8,128)}, u32[]{:S(2)}) copy-start(s32[64,12]{1,0:T(8,128)} %copy.16.tiles_ref) | copy-start | bytes 9220
  20.7 71.8 %copy-start.4 = (s32[128]{0:T(128)S(1)}, s32[128]{0:T(128)}, u32[]{:S(2)}) copy-start(s32[128]{0:T(128)} %owner_ref.1) | copy-start | bytes 1540
  21.6 0.7 copy-start.3
  84.5 2.2 %collective-permute-start.2 = (bf16[16,128,128]{2,1,0:T(8,128)(2,1)}, bf16[16,128,128]{2,1,0:T(8,128)(2,1)S(1)}, u32[]{:S(2)}, u32[]{:S(2)}) collective-permute-start(bf16[16,128,128]{2,1,0:T(8,128)(2,1)} %get-tuple-element.18), channel_id=1, source_target_pairs={{0,8},{8,0},{16,24},{24,16},{1,9},{9,1},{17,25},{25,17},{2,10},{10... | collective-permute-start | bytes 1572872 | tf_op jit(solution)/shard_map/ppermute | solution.py:468
  88.8 19.2 %all-to-all-start.1 = ((bf16[16,128,128]{2,1,0:T(8,128)(2,1)}), bf16[16,128,128]{2,1,0:T(8,128)(2,1)S(1)}, u32[]{:S(2)}, u32[]{:S(2)}) async-start(bf16[16,128,128]{2,1,0:T(8,128)(2,1)} %add_convert_fusion), calls=%async_computation.1 | async-start | bytes 1048576 | tf_op jit(solution)/shard_map/all_to_all | solution.py:472

commit v3 on v2

--- a/solution.py
+++ b/solution.py
@@ -96,10 +96,12 @@
     m = lax.broadcasted_iota(jnp.int32, (count, inner), 0)
     n, m = (lax.rem(n, outer), lax.div(m, outer)) if across else (lax.div(n, inner), lax.rem(m, inner))
     of_row = jnp.where(lax.broadcasted_iota(jnp.int32, (count, outer), 1) == n, 1.0, 0.0)
+    halves = jnp.concatenate([lax.div(table, 256), lax.rem(table, 256)], axis=1)
     spread = jnp.dot(
-        of_row, table.astype(jnp.float32), precision=lax.Precision.HIGHEST,
+        of_row.astype(jnp.bfloat16), halves.astype(jnp.float32).astype(jnp.bfloat16),
         preferred_element_type=jnp.float32,
     )
+    spread = 256.0 * spread[:, :inner] + spread[:, inner:]
     kept = jnp.where(lax.broadcasted_iota(jnp.int32, (count, inner), 1) == m, spread, 0.0)
     number = jnp.sum(kept, axis=1, keepdims=True).astype(jnp.int32)
     choice = lax.broadcasted_iota(jnp.int32, (count, held.shape[0]), 1) == number
@@ -116,6 +118,7 @@
     return pl.pallas_call(
         route_kernel,
         out_shape=jax.ShapeDtypeStruct(table.shape[2:] + held.shape[2:], held.dtype),
+        compiler_params=pltpu.CompilerParams(vmem_limit_bytes=61 << 20),
         name="routed",
     )(table, held)
 
@@ -148,6 +151,7 @@
     return pl.pallas_call(
         beam_kernel,
         out_shape=jax.ShapeDtypeStruct((centres, PARTS * STEPS, LANES), jnp.float32),
+        compiler_params=pltpu.CompilerParams(vmem_limit_bytes=16 << 20),
         name="beams",
     )(slots, arrived, real, imag)
 
@@ -326,9 +330,10 @@
     scalars = pl.BlockSpec(memory_space=pltpu.SMEM)
     inside = pl.BlockSpec(memory_space=pltpu.VMEM)
     outside = pl.BlockSpec(memory_space=pltpu.HBM)
+    anywhere = pl.BlockSpec(memory_space=pl.ANY)
     return pl.pallas_call(
         first_kernel,
-        in_specs=[scalars] * 2 + [outside] * 4,
+        in_specs=[scalars] * 2 + [outside, anywhere, outside, outside],
         out_specs=[inside, inside],
         scratch_shapes=[
             pltpu.VMEM((4,) + tables[0].shape[1:], jnp.float32),
@@ -338,6 +343,7 @@
             jax.ShapeDtypeStruct((2, 4, cells, LANES), jnp.float32),
             jax.ShapeDtypeStruct((SPANS + 1, 2, DIRECTIONS, across), jnp.float32),
         ],
+        compiler_params=pltpu.CompilerParams(vmem_limit_bytes=61 << 20),
         name="first_of",
     )(foot_count, ray_index, *tables)
 
@@ -346,7 +352,7 @@
     count_ref, index_ref, tiles_ref, owner_ref, first_start, first_side, own_beam, other_beam,
     own_ref, other_ref, lateral_ref, spread_ref, mine_ref, theirs_ref, image_ref, start_ref,
     state_ref, side_ref, chain_ref, depth_even, depth_odd, lateral_even, lateral_odd, times_ref,
-    sems,
+    beams_ref, sems, first_sems,
 ):
     group, side = lax.axis_index("beam"), lax.rem(lax.axis_index("shot"), 2)
     groups = lax.axis_size("beam")
@@ -384,7 +390,7 @@
         fetch(after, slot)
         tile = tile_of(entry)
         one_entry(
-            entry[0], tile, last, times_ref.at[1 - slot], (own_beam, other_beam), image_ref,
+            entry[0], tile, last, times_ref.at[1 - slot], (beams_ref.at[0], beams_ref.at[1]), image_ref,
             start_ref, state_ref, side_ref, chain_ref, depth_factors, lateral_factors,
         )
         return later, after, tile
@@ -392,16 +398,27 @@
     first = first_entry(count_ref)
     second = steps_on(first, count_ref)
     fetch(second, 1)
+    arriving = [
+        pltpu.make_async_copy(source, target, first_sems.at[n])
+        for n, (source, target) in enumerate(
+            (
+                (own_beam, beams_ref.at[0]), (other_beam, beams_ref.at[1]),
+                (first_start, start_ref), (first_side, side_ref),
+            )
+        )
+    ]
+    for copy in arriving:
+        copy.start()
     image_ref[...] = jnp.zeros_like(image_ref)
     depth_odd[...] = jnp.zeros_like(depth_odd)
     lateral_odd[...] = jnp.zeros_like(lateral_odd)
-    start_ref[...] = first_start[...]
-    side_ref[...] = first_side[...]
+    for copy in arriving:
+        copy.wait()
     _, later, last = lax.fori_loop(0, count, one, (first, second, jnp.int32(0)))
     arrive(later, lax.rem(count + 1, 2))
     part = product(CHUNKS - 1, depth_factors, lateral_factors)
     image_ref[last] = image_ref[last] + part
-    mine_ref[...] = image_ref[:half]
+    mine_ref[...] = image_ref[:half].astype(mine_ref.dtype)
     theirs_ref[...] = image_ref[half:].astype(theirs_ref.dtype)
 
 
@@ -410,9 +427,10 @@
     scalars = pl.BlockSpec(memory_space=pltpu.SMEM)
     inside = pl.BlockSpec(memory_space=pltpu.VMEM)
     outside = pl.BlockSpec(memory_space=pltpu.HBM)
+    anywhere = pl.BlockSpec(memory_space=pl.ANY)
     return pl.pallas_call(
         tile_kernel,
-        in_specs=[scalars] * 4 + [inside] * 4 + [outside] * 4,
+        in_specs=[scalars] * 4 + [anywhere] * 4 + [outside, anywhere, outside, outside],
         out_specs=[inside] * 2,
         scratch_shapes=[
             pltpu.VMEM((2 * tiles, cells, across), jnp.float32),
@@ -425,18 +443,34 @@
             pltpu.VMEM((CHUNK_STEPS * BLOCK, across), jnp.bfloat16),
             pltpu.VMEM((CHUNK_STEPS * BLOCK, across), jnp.bfloat16),
             pltpu.VMEM((2, 4) + tables[0].shape[1:], jnp.float32),
+            pltpu.VMEM((2,) + beams[0].shape, jnp.float32),
             pltpu.SemaphoreType.DMA((2, 4)),
+            pltpu.SemaphoreType.DMA((4,)),
         ],
         out_shape=[
             jax.ShapeDtypeStruct((tiles, cells, across), kind)
-            for kind in (jnp.float32, jnp.bfloat16)
+            for kind in (jnp.bfloat16, jnp.bfloat16)
         ],
-        compiler_params=pltpu.CompilerParams(vmem_limit_bytes=60 << 20),
+        compiler_params=pltpu.CompilerParams(vmem_limit_bytes=61 << 20),
         cost_estimate=pl.CostEstimate(
             flops=40_000_000_000, transcendentals=0, bytes_accessed=4_000_000
         ),
         name="tiles_of",
     )(*entries, *firsts, *beams, *tables)
+
+
+def add_kernel(one_ref, other_ref, out_ref):
+    total = one_ref[...].astype(jnp.float32) + other_ref[...].astype(jnp.float32)
+    out_ref[...] = total.astype(out_ref.dtype)
+
+
+def added(one, other):
+    return pl.pallas_call(
+        add_kernel,
+        out_shape=jax.ShapeDtypeStruct(one.shape, one.dtype),
+        compiler_params=pltpu.CompilerParams(vmem_limit_bytes=16 << 20),
+        name="added",
+    )(one, other)
 
 
 def body(
@@ -465,12 +499,13 @@
     other_beam = lax.ppermute(own_beam, "shot", swap)
 
     image, theirs = tiles_of(entries, firsts, (own_beam, other_beam), tables, pairs * groups)
-    image = image + lax.ppermute(theirs, "shot", swap).astype(jnp.float32)
+    theirs = lax.ppermute(theirs, "shot", swap)
+    image = added(image, theirs)
     same_side = [
         [(2 * q + c) * groups + n for q in range(pairs) for n in range(groups)] for c in range(2)
     ]
     received = lax.all_to_all(
-        image.astype(jnp.bfloat16), ("shot", "beam"), split_axis=0, concat_axis=0, tiled=True,
+        image, ("shot", "beam"), split_axis=0, concat_axis=0, tiled=True,
         axis_index_groups=same_side,
     )
 

time: 110 us -> 107 us (0.973)
  other arithmetic: 3.59 us -> 1.44 us
    convert_element_type x1 -> x0, other arithmetic: 2.15 us -> none  [body(): image.astype(jnp.bfloat16)]
    pallas_call x1, Pallas kernels: 3.21 us -> 1.48 us  [beams(): pl.pallas_call(beam_kernel, out_shape=jax.ShapeDtypeStruct((centres, PART...]
    pallas_call x2 -> x3, Pallas kernels: 64.9 us -> 66.1 us  [the longest x1 62.5 us: tiles_of(): pl.pallas_call(tile_kernel, in_specs=[scalars] * 4 + [anywhere] * 4 + [ou...]
    unnamed x11 -> x19, local copies, waits for them, and re-layouts: 1.97 us -> 2.43 us
where the time goes in v3:
time: 107 us
  Pallas kernels  69.6 us (65%)
  waiting for transfers between devices  21.8 us (20%)
  starting transfers between devices  11.1 us (10%)
  local copies, waits for them, and re-layouts  2.5 us (2%)
  other arithmetic  1.44 us (1%)
    pallas_call x1, Pallas kernels, tiles_of(): pl.pallas_call(tile_kernel, in_specs=[scalars] * 4 + [anywhere] * 4 + [ou...  62.5 us
    all_to_all x1, waiting for transfers between devices, body(): lax.all_to_all(image, ('shot', 'beam'), split_axis=0, concat_axis=0, tile...  15.1 us
    all_to_all x1, starting transfers between devices, body(): lax.all_to_all(sent, 'beam', split_axis=0, concat_axis=0, tiled=True)  6.83 us
    all_to_all x1, waiting for transfers between devices, body(): lax.all_to_all(sent, 'beam', split_axis=0, concat_axis=0, tiled=True)  4.11 us
    all_to_all x1, starting transfers between devices, body(): lax.all_to_all(image, ('shot', 'beam'), split_axis=0, concat_axis=0, tile...  3.57 us
    pallas_call x1, Pallas kernels, first_of(): pl.pallas_call(first_kernel, in_specs=[scalars] * 2 + [outside, anywhere,...  2.73 us
    unnamed x19, local copies, waits for them, and re-layouts  2.43 us
  transfers between devices with their start and end apart: 5, of which 4 were waited for; matrix products, arithmetic and copies ran while one was open for 1% of the time, Pallas kernels for 4%

profile of v3, /device:TPU:0, one launch (start us, length us, event | category | flops | bytes accessed | tf_op | source)
XLA Modules:
  0.0 106.6 jit_solution(15572664172389691523)
XLA Ops:
  0.0 0.5 collective-permute-start
  0.5 2.0 %routed.1 = bf16[8,32,128]{2,1,0:T(8,128)(2,1)} custom-call(s32[1,8,8,32]{3,2,1,0:T(8,128)} %table_ref.1, bf16[1,256,128]{2,1,0:T(8,128)(2,1)} %held_ref.1), custom_call_target="tpu_custom_call" | custom-call | tf_op jit(solution)/shard_map/routed/pallas_call | solution.py:118
  2.5 6.8 %all-to-all-start = ((bf16[8,32,128]{2,1,0:T(8,128)(2,1)}), bf16[8,32,128]{2,1,0:T(8,128)(2,1)S(1)}, u32[]{:S(2)}, u32[]{:S(2)}) async-start(bf16[8,32,128]{2,1,0:T(8,128)(2,1)} %routed.1), calls=%async_computation | async-start | bytes 131072 | tf_op jit(solution)/shard_map/all_to_all | solution.py:492
  9.3 0.0 copy-start.1
  9.3 0.0 copy-start.2
  9.3 0.0 copy-start.4
  9.4 0.0 copy-start.6
  9.4 0.0 collective-permute-done.other_ref
  9.4 2.7 %first_of.1 = (f32[2,4,128,128]{3,2,1,0:T(8,128)}, f32[5,2,32,128]{3,2,1,0:T(8,128)}) custom-call(s32[1,8]{1,0:T(1,128)} %count_ref.3, s32[8,12]{1,0:T(8,128)} %index_ref.3, f32[256,32,128]{2,1,0:T(8,128)} %bitcast.6, f32[256,32,128]{2,1,0:T(8,128)} %collective-permute-done.other_ref, f32[256,32,128]{2,1,0:T(8,128)} %lateral_ref.3, f32[256,32,128]{2,1,0:T(8,128)} %spread_ref.3), custom_call_target="tpu_custom_call" | custom-call | tf_op jit(solution)/shard_map/first_of/pallas_call | solution.py:334
  12.1 4.1 %all-to-all-done = bf16[8,32,128]{2,1,0:T(8,128)(2,1)S(1)} async-done(((bf16[8,32,128]{2,1,0:T(8,128)(2,1)}), bf16[8,32,128]{2,1,0:T(8,128)(2,1)S(1)}, u32[]{:S(2)}, u32[]{:S(2)}) %all-to-all-start) | async-done | bytes 65568 | tf_op jit(solution)/shard_map/all_to_all | solution.py:492
  16.2 0.0 copy-done.1
  16.2 0.0 copy-done.2
  16.2 0.0 copy-done.4
  16.2 1.5 %beams.1.own_beam = f32[8,32,128]{2,1,0:T(8,128)S(1)} custom-call(s32[1,8,32]{2,1,0:T(8,128)S(1)} %copy-done.4, bf16[256,128]{1,0:T(8,128)(2,1)S(1)} %bitcast.4, f32[16,32,128]{2,1,0:T(8,128)S(1)} %copy-done.1, f32[16,32,128]{2,1,0:T(8,128)S(1)} %copy-done.2), custom_call_target="tpu_custom_call" | custom-call | tf_op jit(solution)/shard_map/beams/pallas_call | solution.py:151
  17.7 0.0 copy-start.3
  17.7 0.1 collective-permute-start.1
  17.8 0.0 copy-done.6
  17.8 0.7 copy.16.tiles_ref
  18.5 0.0 copy-start.5
  18.5 0.0 copy-start.8
  18.5 0.6 collective-permute-done.1.other_beam
  19.2 0.0 copy-done.3
  19.2 0.0 copy-start.7
  19.2 0.7 copy-done.7
  19.8 62.5 %tiles_of.1 = (bf16[16,128,128]{2,1,0:T(8,128)(2,1)}, bf16[16,128,128]{2,1,0:T(8,128)(2,1)}) custom-call(s32[1,8]{1,0:T(1,128)} %count_ref.3, s32[8,12]{1,0:T(8,128)} %index_ref.3, s32[64,12]{1,0:T(8,128)} %copy.16.tiles_ref, s32[128]{0:T(128)} %owner_ref.1, f32[2,4,128,128]{3,2,1,0:T(8,128)} %get-tuple-element.14.first_start, ...), custom_call_target="tpu_custom_call" | custom-call | flops 40000000000 | bytes 4000000 | tf_op jit(solution)/shard_map/tiles_of/pallas_call | solution.py:431
  82.3 0.2 collective-permute-start.2
  82.5 2.0 %collective-permute-done.2.other_ref = bf16[16,128,128]{2,1,0:T(8,128)(2,1)S(1)} collective-permute-done((bf16[16,128,128]{2,1,0:T(8,128)(2,1)}, bf16[16,128,128]{2,1,0:T(8,128)(2,1)S(1)}, u32[]{:S(2)}, u32[]{:S(2)}) %collective-permute-start.2) | collective-permute-done | bytes 524320 | tf_op jit(solution)/shard_map/ppermute | solution.py:502
  84.5 0.0 copy-start
  84.5 1.0 copy-done
  85.5 0.9 added.1
  86.4 3.6 %all-to-all-start.1 = ((bf16[16,128,128]{2,1,0:T(8,128)(2,1)}), bf16[16,128,128]{2,1,0:T(8,128)(2,1)S(1)}, u32[]{:S(2)}, u32[]{:S(2)}) async-start(bf16[16,128,128]{2,1,0:T(8,128)(2,1)} %added.1), calls=%async_computation.1 | async-start | bytes 1048576 | tf_op jit(solution)/shard_map/all_to_all | solution.py:507
  90.0 0.0 copy-done.5
  90.0 0.1 eq.38
  90.1 0.0 copy-done.8
  90.1 0.1 convert_reduce_fusion.1
  90.2 0.2 fusion
  90.4 0.1 select_reduce_fusion.1
  90.5 15.1 %all-to-all-done.1 = bf16[16,128,128]{2,1,0:T(8,128)(2,1)S(1)} async-done(((bf16[16,128,128]{2,1,0:T(8,128)(2,1)}), bf16[16,128,128]{2,1,0:T(8,128)(2,1)S(1)}, u32[]{:S(2)}, u32[]{:S(2)}) %all-to-all-start.1) | async-done | bytes 524320 | tf_op jit(solution)/shard_map/all_to_all | solution.py:507
  105.6 0.1 convert_reduce_fusion
  105.7 0.9 select_reduce_fusion
  (2 shorter events, 0.0 us)
Async XLA Ops:
  0.0 9.4 %collective-permute-start = (f32[256,32,128]{2,1,0:T(8,128)}, f32[256,32,128]{2,1,0:T(8,128)}, u32[]{:S(2)}, u32[]{:S(2)}) collective-permute-start(f32[256,32,128]{2,1,0:T(8,128)} %bitcast.5), channel_id=1, source_target_pairs={{0,8},{8,0},{16,24},{24,16},{1,9},{9,1},{17,25},{25,17},{2,10},{10... | collective-permute-start | bytes 12582920 | tf_op jit(solution)/shard_map/ppermute | solution.py:489
  2.5 13.7 %all-to-all-start = ((bf16[8,32,128]{2,1,0:T(8,128)(2,1)}), bf16[8,32,128]{2,1,0:T(8,128)(2,1)S(1)}, u32[]{:S(2)}, u32[]{:S(2)}) async-start(bf16[8,32,128]{2,1,0:T(8,128)(2,1)} %routed.1), calls=%async_computation | async-start | bytes 131072 | tf_op jit(solution)/shard_map/all_to_all | solution.py:492
  9.3 6.9 %copy-start.1 = (f32[16,32,128]{2,1,0:T(8,128)S(1)}, f32[16,32,128]{2,1,0:T(8,128)}, u32[]{:S(2)}) copy-start(f32[16,32,128]{2,1,0:T(8,128)} %constant.20.clone.real_ref) | copy-start | bytes 786436
  9.3 6.9 %copy-start.2 = (f32[16,32,128]{2,1,0:T(8,128)S(1)}, f32[16,32,128]{2,1,0:T(8,128)}, u32[]{:S(2)}) copy-start(f32[16,32,128]{2,1,0:T(8,128)} %constant.21.clone.imag_ref) | copy-start | bytes 786436
  9.3 6.9 %copy-start.4 = (s32[1,8,32]{2,1,0:T(8,128)S(1)}, s32[1,8,32]{2,1,0:T(8,128)}, u32[]{:S(2)}) copy-start(s32[1,8,32]{2,1,0:T(8,128)} %slot_ref.1) | copy-start | bytes 3076
  9.4 8.5 %copy-start.6 = (s32[64,12]{0,1:T(8,128)S(1)}, s32[64,12]{0,1:T(8,128)}, u32[]{:S(2)}) copy-start(s32[64,12]{0,1:T(8,128)} %param.20) | copy-start | bytes 9220
  17.7 1.4 %copy-start.3 = (f32[8,32,128]{2,1,0:T(8,128)}, f32[8,32,128]{2,1,0:T(8,128)S(1)}, u32[]{:S(2)}) copy-start(f32[8,32,128]{2,1,0:T(8,128)S(1)} %beams.1.own_beam) | copy-start | bytes 393220
  17.7 1.4 %collective-permute-start.1 = (f32[8,32,128]{2,1,0:T(8,128)S(1)}, f32[8,32,128]{2,1,0:T(8,128)S(1)}, u32[]{:S(2)}, u32[]{:S(2)}) collective-permute-start(f32[8,32,128]{2,1,0:T(8,128)S(1)} %beams.1.own_beam), channel_id=1, source_target_pairs={{0,8},{8,0},{16,24},{24,16},{1,9},{9,1},{17,25},{25,17},{2,10},{10... | collective-permute-start | bytes 393224 | tf_op jit(solution)/shard_map/ppermute | solution.py:499
  18.5 71.5 %copy-start.5 = (s32[64,12]{1,0:T(8,128)S(1)}, s32[64,12]{1,0:T(8,128)}, u32[]{:S(2)}) copy-start(s32[64,12]{1,0:T(8,128)} %copy.16.tiles_ref) | copy-start | bytes 9220
  18.5 71.6 %copy-start.8 = (s32[128]{0:T(128)S(1)}, s32[128]{0:T(128)}, u32[]{:S(2)}) copy-start(s32[128]{0:T(128)} %owner_ref.1) | copy-start | bytes 1540
  19.2 0.7 copy-start.7
  82.3 2.2 %collective-permute-start.2 = (bf16[16,128,128]{2,1,0:T(8,128)(2,1)}, bf16[16,128,128]{2,1,0:T(8,128)(2,1)S(1)}, u32[]{:S(2)}, u32[]{:S(2)}) collective-permute-start(bf16[16,128,128]{2,1,0:T(8,128)(2,1)} %get-tuple-element.18), channel_id=1, source_target_pairs={{0,8},{8,0},{16,24},{24,16},{1,9},{9,1},{17,25},{25,17},{2,10},{10... | collective-permute-start | bytes 1572872 | tf_op jit(solution)/shard_map/ppermute | solution.py:502
  84.5 1.0 copy-start
  86.4 19.2 %all-to-all-start.1 = ((bf16[16,128,128]{2,1,0:T(8,128)(2,1)}), bf16[16,128,128]{2,1,0:T(8,128)(2,1)S(1)}, u32[]{:S(2)}, u32[]{:S(2)}) async-start(bf16[16,128,128]{2,1,0:T(8,128)(2,1)} %added.1), calls=%async_computation.1 | async-start | bytes 1048576 | tf_op jit(solution)/shard_map/all_to_all | solution.py:507

commit v4 on v3

--- a/solution.py
+++ b/solution.py
@@ -357,7 +357,7 @@
     group, side = lax.axis_index("beam"), lax.rem(lax.axis_index("shot"), 2)
     groups = lax.axis_size("beam")
     half = mine_ref.shape[0]
-    centres = index_ref.shape[0]
+    centres, slots = index_ref.shape
     found = count_ref[0, 0]
     for n in range(1, centres):
         found = found + count_ref[0, n]
@@ -377,7 +377,7 @@
             copy.wait()
 
     def tile_of(entry):
-        owner = owner_ref[tiles_ref[group * centres + entry[0], entry[1]]]
+        owner = owner_ref[tiles_ref[(group * centres + entry[0]) * slots + entry[1]]]
         shot, home = lax.div(owner, groups), lax.rem(owner, groups)
         away = jnp.where(lax.rem(shot, 2) == side, 0, half)
         return lax.div(shot, 2) * groups + home + away
@@ -451,7 +451,7 @@
             jax.ShapeDtypeStruct((tiles, cells, across), kind)
             for kind in (jnp.bfloat16, jnp.bfloat16)
         ],
-        compiler_params=pltpu.CompilerParams(vmem_limit_bytes=61 << 20),
+        compiler_params=pltpu.CompilerParams(vmem_limit_bytes=50 << 20),
         cost_estimate=pl.CostEstimate(
             flops=40_000_000_000, transcendentals=0, bytes_accessed=4_000_000
         ),
@@ -493,8 +493,10 @@
     arrived = arrived.reshape(-1, arrived.shape[-1])
     tables = (own_depth, other_depth, ray_lateral, ray_spread)
     firsts = first_of(foot_count, ray_index, tables)
-    entries = (foot_count, ray_index, foot_tiles, tile_owner)
-    arrived, firsts = lax.optimization_barrier((arrived, firsts))
+    arrived, firsts, flat_tiles = lax.optimization_barrier(
+        (arrived, firsts, foot_tiles.reshape(-1))
+    )
+    entries = (foot_count, ray_index, flat_tiles, tile_owner)
     own_beam = beams(window_slots, arrived, window_slots.shape[1])
     other_beam = lax.ppermute(own_beam, "shot", swap)
 

time: 107 us -> 106 us (level)
  Pallas kernels: 69.6 us -> 67.7 us
    pallas_call x1, Pallas kernels: 62.5 us -> 60.5 us  [tiles_of(): pl.pallas_call(tile_kernel, in_specs=[scalars] * 4 + [anywhere] * 4 + [ou...]
    unnamed x19 -> x17, local copies, waits for them, and re-layouts: 2.43 us -> 2.77 us
  transfers between devices with their start and end apart: 5 -> 5, of which waited for: 4 -> 4; matrix products, arithmetic and copies ran while one was open for 1% -> 1% of each run, Pallas kernels for 4% -> 5%
where the time goes in v4:
time: 106 us; the launch traced here: 105 us
  Pallas kernels  67.7 us (64%)
  waiting for transfers between devices  21.3 us (20%)
  starting transfers between devices  11.4 us (11%)
  local copies, waits for them, and re-layouts  2.95 us (3%)
  other arithmetic  1.44 us (1%)
    pallas_call x1, Pallas kernels, tiles_of(): pl.pallas_call(tile_kernel, in_specs=[scalars] * 4 + [anywhere] * 4 + [ou...  60.5 us
    all_to_all x1, waiting for transfers between devices, body(): lax.all_to_all(image, ('shot', 'beam'), split_axis=0, concat_axis=0, tile...  15 us
    all_to_all x1, starting transfers between devices, body(): lax.all_to_all(sent, 'beam', split_axis=0, concat_axis=0, tiled=True)  6.83 us
    all_to_all x1, starting transfers between devices, body(): lax.all_to_all(image, ('shot', 'beam'), split_axis=0, concat_axis=0, tile...  3.85 us
    all_to_all x1, waiting for transfers between devices, body(): lax.all_to_all(sent, 'beam', split_axis=0, concat_axis=0, tiled=True)  3.2 us
    unnamed x17, local copies, waits for them, and re-layouts  2.77 us
    pallas_call x1, Pallas kernels, first_of(): pl.pallas_call(first_kernel, in_specs=[scalars] * 2 + [outside, anywhere,...  2.72 us
  transfers between devices with their start and end apart: 5, of which 4 were waited for; matrix products, arithmetic and copies ran while one was open for 1% of the time, Pallas kernels for 5%

profile of v4, /device:TPU:0, one launch (start us, length us, event | category | flops | bytes accessed | tf_op | source)
XLA Modules:
  0.0 104.9 jit_solution(2203730204395675916)
XLA Ops:
  0.0 0.5 collective-permute-start
  0.5 2.0 %routed.1 = bf16[8,32,128]{2,1,0:T(8,128)(2,1)} custom-call(s32[1,8,8,32]{3,2,1,0:T(8,128)} %table_ref.1, bf16[1,256,128]{2,1,0:T(8,128)(2,1)} %held_ref.1), custom_call_target="tpu_custom_call" | custom-call | tf_op jit(solution)/shard_map/routed/pallas_call | solution.py:118
  2.5 6.8 %all-to-all-start = ((bf16[8,32,128]{2,1,0:T(8,128)(2,1)}), bf16[8,32,128]{2,1,0:T(8,128)(2,1)S(1)}, u32[]{:S(2)}, u32[]{:S(2)}) async-start(bf16[8,32,128]{2,1,0:T(8,128)(2,1)} %routed.1), calls=%async_computation | async-start | bytes 131072 | tf_op jit(solution)/shard_map/all_to_all | solution.py:492
  9.3 0.8 copy.15
  10.1 0.1 reshape.33.tiles_ref
  10.2 0.0 copy-start
  10.2 0.0 copy-start.1
  10.2 0.0 copy-start.2
  10.3 0.0 copy-start.3
  10.3 0.0 copy-start.4
  10.3 0.0 copy-start.7
  10.3 0.0 collective-permute-done.other_ref
  10.3 2.7 %first_of.1 = (f32[2,4,128,128]{3,2,1,0:T(8,128)}, f32[5,2,32,128]{3,2,1,0:T(8,128)}) custom-call(s32[1,8]{1,0:T(1,128)} %count_ref.3, s32[8,12]{1,0:T(8,128)} %index_ref.3, f32[256,32,128]{2,1,0:T(8,128)} %bitcast.6, f32[256,32,128]{2,1,0:T(8,128)} %collective-permute-done.other_ref, f32[256,32,128]{2,1,0:T(8,128)} %lateral_ref.3, f32[256,32,128]{2,1,0:T(8,128)} %spread_ref.3), custom_call_target="tpu_custom_call" | custom-call | tf_op jit(solution)/shard_map/first_of/pallas_call | solution.py:334
  13.0 3.2 %all-to-all-done = bf16[8,32,128]{2,1,0:T(8,128)(2,1)S(1)} async-done(((bf16[8,32,128]{2,1,0:T(8,128)(2,1)}), bf16[8,32,128]{2,1,0:T(8,128)(2,1)S(1)}, u32[]{:S(2)}, u32[]{:S(2)}) %all-to-all-start) | async-done | bytes 65568 | tf_op jit(solution)/shard_map/all_to_all | solution.py:492
  16.2 0.0 copy-done
  16.2 0.0 copy-done.1
  16.2 0.0 copy-done.2
  16.2 1.5 %beams.1.own_beam = f32[8,32,128]{2,1,0:T(8,128)S(1)} custom-call(s32[1,8,32]{2,1,0:T(8,128)S(1)} %copy-done.2, bf16[256,128]{1,0:T(8,128)(2,1)S(1)} %bitcast.4, f32[16,32,128]{2,1,0:T(8,128)S(1)} %copy-done.1, f32[16,32,128]{2,1,0:T(8,128)S(1)} %copy-done), custom_call_target="tpu_custom_call" | custom-call | tf_op jit(solution)/shard_map/beams/pallas_call | solution.py:151
  17.7 0.1 collective-permute-start.1
  17.8 1.3 %collective-permute-done.1.other_beam = f32[8,32,128]{2,1,0:T(8,128)S(1)} collective-permute-done((f32[8,32,128]{2,1,0:T(8,128)S(1)}, f32[8,32,128]{2,1,0:T(8,128)S(1)}, u32[]{:S(2)}, u32[]{:S(2)}) %collective-permute-start.1) | collective-permute-done | bytes 131104 | tf_op jit(solution)/shard_map/ppermute | solution.py:501
  19.1 0.0 copy-done.3
  19.2 0.0 copy-done.4
  19.2 0.0 copy-done.7
  19.2 0.0 copy-start.5
  19.2 1.0 copy-done.5
  20.2 0.0 copy-start.6
  20.2 0.9 copy-done.6
  21.1 60.5 %tiles_of.1 = (bf16[16,128,128]{2,1,0:T(8,128)(2,1)S(1)}, bf16[16,128,128]{2,1,0:T(8,128)(2,1)S(1)}) custom-call(s32[1,8]{1,0:T(1,128)S(1)} %copy-done.4, s32[8,12]{1,0:T(8,128)S(1)} %copy-done.3, s32[768]{0:T(1024)S(1)} %reshape.33.tiles_ref, s32[128]{0:T(128)S(1)} %copy-done.7, f32[2,4,128,128]{3,2,1,0:T(8,128)S(1)} %copy-done.5, ...), custom_call_target="tpu_custom_call" | custom-call | flops 40000000000 | bytes 4000000 | tf_op jit(solution)/shard_map/tiles_of/pallas_call | solution.py:431
  81.6 0.2 collective-permute-start.2
  81.8 1.8 %collective-permute-done.2.other_ref = bf16[16,128,128]{2,1,0:T(8,128)(2,1)S(1)} collective-permute-done((bf16[16,128,128]{2,1,0:T(8,128)(2,1)S(1)}, bf16[16,128,128]{2,1,0:T(8,128)(2,1)S(1)}, u32[]{:S(2)}, u32[]{:S(2)}) %collective-permute-start.2) | collective-permute-done | bytes 524320 | tf_op jit(solution)/shard_map/ppermute | solution.py:504
  83.6 0.9 added.1
  84.5 3.9 %all-to-all-start.1 = ((bf16[16,128,128]{2,1,0:T(8,128)(2,1)}), bf16[16,128,128]{2,1,0:T(8,128)(2,1)S(1)}, u32[]{:S(2)}, u32[]{:S(2)}) async-start(bf16[16,128,128]{2,1,0:T(8,128)(2,1)} %added.1), calls=%async_computation.1 | async-start | bytes 1048576 | tf_op jit(solution)/shard_map/all_to_all | solution.py:509
  88.4 0.1 eq.38
  88.5 0.1 convert_reduce_fusion.1
  88.6 0.2 fusion
  88.8 0.1 select_reduce_fusion.1
  88.9 15.0 %all-to-all-done.1 = bf16[16,128,128]{2,1,0:T(8,128)(2,1)S(1)} async-done(((bf16[16,128,128]{2,1,0:T(8,128)(2,1)}), bf16[16,128,128]{2,1,0:T(8,128)(2,1)S(1)}, u32[]{:S(2)}, u32[]{:S(2)}) %all-to-all-start.1) | async-done | bytes 524320 | tf_op jit(solution)/shard_map/all_to_all | solution.py:509
  103.9 0.1 convert_reduce_fusion
  104.0 0.9 select_reduce_fusion
  (2 shorter events, 0.0 us)
Async XLA Ops:
  0.0 10.3 %collective-permute-start = (f32[256,32,128]{2,1,0:T(8,128)}, f32[256,32,128]{2,1,0:T(8,128)}, u32[]{:S(2)}, u32[]{:S(2)}) collective-permute-start(f32[256,32,128]{2,1,0:T(8,128)} %bitcast.5), channel_id=1, source_target_pairs={{0,8},{8,0},{16,24},{24,16},{1,9},{9,1},{17,25},{25,17},{2,10},{10... | collective-permute-start | bytes 12582920 | tf_op jit(solution)/shard_map/ppermute | solution.py:489
  2.5 13.7 %all-to-all-start = ((bf16[8,32,128]{2,1,0:T(8,128)(2,1)}), bf16[8,32,128]{2,1,0:T(8,128)(2,1)S(1)}, u32[]{:S(2)}, u32[]{:S(2)}) async-start(bf16[8,32,128]{2,1,0:T(8,128)(2,1)} %routed.1), calls=%async_computation | async-start | bytes 131072 | tf_op jit(solution)/shard_map/all_to_all | solution.py:492
  10.2 6.0 %copy-start = (f32[16,32,128]{2,1,0:T(8,128)S(1)}, f32[16,32,128]{2,1,0:T(8,128)}, u32[]{:S(2)}) copy-start(f32[16,32,128]{2,1,0:T(8,128)} %constant.21.clone.imag_ref) | copy-start | bytes 786436
  10.2 6.0 %copy-start.1 = (f32[16,32,128]{2,1,0:T(8,128)S(1)}, f32[16,32,128]{2,1,0:T(8,128)}, u32[]{:S(2)}) copy-start(f32[16,32,128]{2,1,0:T(8,128)} %constant.20.clone.real_ref) | copy-start | bytes 786436
  10.2 6.0 %copy-start.2 = (s32[1,8,32]{2,1,0:T(8,128)S(1)}, s32[1,8,32]{2,1,0:T(8,128)}, u32[]{:S(2)}) copy-start(s32[1,8,32]{2,1,0:T(8,128)} %slot_ref.1) | copy-start | bytes 3076
  10.3 8.9 %copy-start.3 = (s32[8,12]{1,0:T(8,128)S(1)}, s32[8,12]{1,0:T(8,128)}, u32[]{:S(2)}) copy-start(s32[8,12]{1,0:T(8,128)} %index_ref.3) | copy-start | bytes 1156
  10.3 8.9 %copy-start.4 = (s32[1,8]{1,0:T(1,128)S(1)}, s32[1,8]{1,0:T(1,128)}, u32[]{:S(2)}) copy-start(s32[1,8]{1,0:T(1,128)} %count_ref.3) | copy-start | bytes 100
  10.3 8.9 %copy-start.7 = (s32[128]{0:T(128)S(1)}, s32[128]{0:T(128)}, u32[]{:S(2)}) copy-start(s32[128]{0:T(128)} %owner_ref.1) | copy-start | bytes 1540
  17.7 1.4 %collective-permute-start.1 = (f32[8,32,128]{2,1,0:T(8,128)S(1)}, f32[8,32,128]{2,1,0:T(8,128)S(1)}, u32[]{:S(2)}, u32[]{:S(2)}) collective-permute-start(f32[8,32,128]{2,1,0:T(8,128)S(1)} %beams.1.own_beam), channel_id=1, source_target_pairs={{0,8},{8,0},{16,24},{24,16},{1,9},{9,1},{17,25},{25,17},{2,10},{10... | collective-permute-start | bytes 393224 | tf_op jit(solution)/shard_map/ppermute | solution.py:501
  19.2 1.0 copy-start.5
  20.2 0.9 copy-start.6
  81.6 2.0 %collective-permute-start.2 = (bf16[16,128,128]{2,1,0:T(8,128)(2,1)S(1)}, bf16[16,128,128]{2,1,0:T(8,128)(2,1)S(1)}, u32[]{:S(2)}, u32[]{:S(2)}) collective-permute-start(bf16[16,128,128]{2,1,0:T(8,128)(2,1)S(1)} %get-tuple-element.20), channel_id=1, source_target_pairs={{0,8},{8,0},{16,24},{24,16},{1,9},{9,1},{17,25},{25,17},{2,10},{10... | collective-permute-start | bytes 1572872 | tf_op jit(solution)/shard_map/ppermute | solution.py:504
  84.5 19.4 %all-to-all-start.1 = ((bf16[16,128,128]{2,1,0:T(8,128)(2,1)}), bf16[16,128,128]{2,1,0:T(8,128)(2,1)S(1)}, u32[]{:S(2)}, u32[]{:S(2)}) async-start(bf16[16,128,128]{2,1,0:T(8,128)(2,1)} %added.1), calls=%async_computation.1 | async-start | bytes 1048576 | tf_op jit(solution)/shard_map/all_to_all | solution.py:509

commit v5 on v4

--- a/solution.py
+++ b/solution.py
@@ -430,7 +430,7 @@
     anywhere = pl.BlockSpec(memory_space=pl.ANY)
     return pl.pallas_call(
         tile_kernel,
-        in_specs=[scalars] * 4 + [anywhere] * 4 + [outside, anywhere, outside, outside],
+        in_specs=[scalars] * 4 + [outside] * 3 + [anywhere, outside, anywhere, outside, outside],
         out_specs=[inside] * 2,
         scratch_shapes=[
             pltpu.VMEM((2 * tiles, cells, across), jnp.float32),

time: 106 us -> 106 us (level)
  no operation moved by 1% of the time
where the time goes in v5:
time: 106 us; the launch traced here: 105 us
  Pallas kernels  67.7 us (64%)
  waiting for transfers between devices  21.3 us (20%)
  starting transfers between devices  11.4 us (11%)
  local copies, waits for them, and re-layouts  2.95 us (3%)
  other arithmetic  1.44 us (1%)
    pallas_call x1, Pallas kernels, tiles_of(): pl.pallas_call(tile_kernel, in_specs=[scalars] * 4 + [outside] * 3 + [any...  60.5 us
    all_to_all x1, waiting for transfers between devices, body(): lax.all_to_all(image, ('shot', 'beam'), split_axis=0, concat_axis=0, tile...  15 us
    all_to_all x1, starting transfers between devices, body(): lax.all_to_all(sent, 'beam', split_axis=0, concat_axis=0, tiled=True)  6.83 us
    all_to_all x1, starting transfers between devices, body(): lax.all_to_all(image, ('shot', 'beam'), split_axis=0, concat_axis=0, tile...  3.85 us
    all_to_all x1, waiting for transfers between devices, body(): lax.all_to_all(sent, 'beam', split_axis=0, concat_axis=0, tiled=True)  3.2 us
    unnamed x17, local copies, waits for them, and re-layouts  2.77 us
    pallas_call x1, Pallas kernels, first_of(): pl.pallas_call(first_kernel, in_specs=[scalars] * 2 + [outside, anywhere,...  2.72 us
  transfers between devices with their start and end apart: 5, of which 4 were waited for; matrix products, arithmetic and copies ran while one was open for 1% of the time, Pallas kernels for 5%

profile of v5, /device:TPU:0, one launch (start us, length us, event | category | flops | bytes accessed | tf_op | source)
XLA Modules:
  0.0 104.9 jit_solution(2203730204395675916)
XLA Ops:
  0.0 0.5 collective-permute-start
  0.5 2.0 %routed.1 = bf16[8,32,128]{2,1,0:T(8,128)(2,1)} custom-call(s32[1,8,8,32]{3,2,1,0:T(8,128)} %table_ref.1, bf16[1,256,128]{2,1,0:T(8,128)(2,1)} %held_ref.1), custom_call_target="tpu_custom_call" | custom-call | tf_op jit(solution)/shard_map/routed/pallas_call | solution.py:118
  2.5 6.8 %all-to-all-start = ((bf16[8,32,128]{2,1,0:T(8,128)(2,1)}), bf16[8,32,128]{2,1,0:T(8,128)(2,1)S(1)}, u32[]{:S(2)}, u32[]{:S(2)}) async-start(bf16[8,32,128]{2,1,0:T(8,128)(2,1)} %routed.1), calls=%async_computation | async-start | bytes 131072 | tf_op jit(solution)/shard_map/all_to_all | solution.py:492
  9.3 0.8 copy.15
  10.1 0.1 reshape.33.tiles_ref
  10.2 0.0 copy-start
  10.2 0.0 copy-start.1
  10.2 0.0 copy-start.2
  10.3 0.0 copy-start.3
  10.3 0.0 copy-start.4
  10.3 0.0 copy-start.7
  10.3 0.0 collective-permute-done.other_ref
  10.3 2.7 %first_of.1 = (f32[2,4,128,128]{3,2,1,0:T(8,128)}, f32[5,2,32,128]{3,2,1,0:T(8,128)}) custom-call(s32[1,8]{1,0:T(1,128)} %count_ref.3, s32[8,12]{1,0:T(8,128)} %index_ref.3, f32[256,32,128]{2,1,0:T(8,128)} %bitcast.6, f32[256,32,128]{2,1,0:T(8,128)} %collective-permute-done.other_ref, f32[256,32,128]{2,1,0:T(8,128)} %lateral_ref.3, f32[256,32,128]{2,1,0:T(8,128)} %spread_ref.3), custom_call_target="tpu_custom_call" | custom-call | tf_op jit(solution)/shard_map/first_of/pallas_call | solution.py:334
  13.0 3.2 %all-to-all-done = bf16[8,32,128]{2,1,0:T(8,128)(2,1)S(1)} async-done(((bf16[8,32,128]{2,1,0:T(8,128)(2,1)}), bf16[8,32,128]{2,1,0:T(8,128)(2,1)S(1)}, u32[]{:S(2)}, u32[]{:S(2)}) %all-to-all-start) | async-done | bytes 65568 | tf_op jit(solution)/shard_map/all_to_all | solution.py:492
  16.2 0.0 copy-done
  16.2 0.0 copy-done.1
  16.2 0.0 copy-done.2
  16.2 1.5 %beams.1.own_beam = f32[8,32,128]{2,1,0:T(8,128)S(1)} custom-call(s32[1,8,32]{2,1,0:T(8,128)S(1)} %copy-done.2, bf16[256,128]{1,0:T(8,128)(2,1)S(1)} %bitcast.4, f32[16,32,128]{2,1,0:T(8,128)S(1)} %copy-done.1, f32[16,32,128]{2,1,0:T(8,128)S(1)} %copy-done), custom_call_target="tpu_custom_call" | custom-call | tf_op jit(solution)/shard_map/beams/pallas_call | solution.py:151
  17.7 0.1 collective-permute-start.1
  17.8 1.3 %collective-permute-done.1.other_beam = f32[8,32,128]{2,1,0:T(8,128)S(1)} collective-permute-done((f32[8,32,128]{2,1,0:T(8,128)S(1)}, f32[8,32,128]{2,1,0:T(8,128)S(1)}, u32[]{:S(2)}, u32[]{:S(2)}) %collective-permute-start.1) | collective-permute-done | bytes 131104 | tf_op jit(solution)/shard_map/ppermute | solution.py:501
  19.1 0.0 copy-done.3
  19.2 0.0 copy-done.4
  19.2 0.0 copy-done.7
  19.2 0.0 copy-start.5
  19.2 1.0 copy-done.5
  20.2 0.0 copy-start.6
  20.2 0.9 copy-done.6
  21.1 60.5 %tiles_of.1 = (bf16[16,128,128]{2,1,0:T(8,128)(2,1)S(1)}, bf16[16,128,128]{2,1,0:T(8,128)(2,1)S(1)}) custom-call(s32[1,8]{1,0:T(1,128)S(1)} %copy-done.4, s32[8,12]{1,0:T(8,128)S(1)} %copy-done.3, s32[768]{0:T(1024)S(1)} %reshape.33.tiles_ref, s32[128]{0:T(128)S(1)} %copy-done.7, f32[2,4,128,128]{3,2,1,0:T(8,128)S(1)} %copy-done.5, ...), custom_call_target="tpu_custom_call" | custom-call | flops 40000000000 | bytes 4000000 | tf_op jit(solution)/shard_map/tiles_of/pallas_call | solution.py:431
  81.6 0.2 collective-permute-start.2
  81.8 1.8 %collective-permute-done.2.other_ref = bf16[16,128,128]{2,1,0:T(8,128)(2,1)S(1)} collective-permute-done((bf16[16,128,128]{2,1,0:T(8,128)(2,1)S(1)}, bf16[16,128,128]{2,1,0:T(8,128)(2,1)S(1)}, u32[]{:S(2)}, u32[]{:S(2)}) %collective-permute-start.2) | collective-permute-done | bytes 524320 | tf_op jit(solution)/shard_map/ppermute | solution.py:504
  83.6 0.9 added.1
  84.5 3.9 %all-to-all-start.1 = ((bf16[16,128,128]{2,1,0:T(8,128)(2,1)}), bf16[16,128,128]{2,1,0:T(8,128)(2,1)S(1)}, u32[]{:S(2)}, u32[]{:S(2)}) async-start(bf16[16,128,128]{2,1,0:T(8,128)(2,1)} %added.1), calls=%async_computation.1 | async-start | bytes 1048576 | tf_op jit(solution)/shard_map/all_to_all | solution.py:509
  88.4 0.1 eq.38
  88.5 0.1 convert_reduce_fusion.1
  88.6 0.2 fusion
  88.8 0.1 select_reduce_fusion.1
  88.9 15.0 %all-to-all-done.1 = bf16[16,128,128]{2,1,0:T(8,128)(2,1)S(1)} async-done(((bf16[16,128,128]{2,1,0:T(8,128)(2,1)}), bf16[16,128,128]{2,1,0:T(8,128)(2,1)S(1)}, u32[]{:S(2)}, u32[]{:S(2)}) %all-to-all-start.1) | async-done | bytes 524320 | tf_op jit(solution)/shard_map/all_to_all | solution.py:509
  103.9 0.1 convert_reduce_fusion
  104.0 0.9 select_reduce_fusion
  (2 shorter events, 0.0 us)
Async XLA Ops:
  0.0 10.3 %collective-permute-start = (f32[256,32,128]{2,1,0:T(8,128)}, f32[256,32,128]{2,1,0:T(8,128)}, u32[]{:S(2)}, u32[]{:S(2)}) collective-permute-start(f32[256,32,128]{2,1,0:T(8,128)} %bitcast.5), channel_id=1, source_target_pairs={{0,8},{8,0},{16,24},{24,16},{1,9},{9,1},{17,25},{25,17},{2,10},{10... | collective-permute-start | bytes 12582920 | tf_op jit(solution)/shard_map/ppermute | solution.py:489
  2.5 13.7 %all-to-all-start = ((bf16[8,32,128]{2,1,0:T(8,128)(2,1)}), bf16[8,32,128]{2,1,0:T(8,128)(2,1)S(1)}, u32[]{:S(2)}, u32[]{:S(2)}) async-start(bf16[8,32,128]{2,1,0:T(8,128)(2,1)} %routed.1), calls=%async_computation | async-start | bytes 131072 | tf_op jit(solution)/shard_map/all_to_all | solution.py:492
  10.2 6.0 %copy-start = (f32[16,32,128]{2,1,0:T(8,128)S(1)}, f32[16,32,128]{2,1,0:T(8,128)}, u32[]{:S(2)}) copy-start(f32[16,32,128]{2,1,0:T(8,128)} %constant.21.clone.imag_ref) | copy-start | bytes 786436
  10.2 6.0 %copy-start.1 = (f32[16,32,128]{2,1,0:T(8,128)S(1)}, f32[16,32,128]{2,1,0:T(8,128)}, u32[]{:S(2)}) copy-start(f32[16,32,128]{2,1,0:T(8,128)} %constant.20.clone.real_ref) | copy-start | bytes 786436
  10.2 6.0 %copy-start.2 = (s32[1,8,32]{2,1,0:T(8,128)S(1)}, s32[1,8,32]{2,1,0:T(8,128)}, u32[]{:S(2)}) copy-start(s32[1,8,32]{2,1,0:T(8,128)} %slot_ref.1) | copy-start | bytes 3076
  10.3 8.9 %copy-start.3 = (s32[8,12]{1,0:T(8,128)S(1)}, s32[8,12]{1,0:T(8,128)}, u32[]{:S(2)}) copy-start(s32[8,12]{1,0:T(8,128)} %index_ref.3) | copy-start | bytes 1156
  10.3 8.9 %copy-start.4 = (s32[1,8]{1,0:T(1,128)S(1)}, s32[1,8]{1,0:T(1,128)}, u32[]{:S(2)}) copy-start(s32[1,8]{1,0:T(1,128)} %count_ref.3) | copy-start | bytes 100
  10.3 8.9 %copy-start.7 = (s32[128]{0:T(128)S(1)}, s32[128]{0:T(128)}, u32[]{:S(2)}) copy-start(s32[128]{0:T(128)} %owner_ref.1) | copy-start | bytes 1540
  17.7 1.4 %collective-permute-start.1 = (f32[8,32,128]{2,1,0:T(8,128)S(1)}, f32[8,32,128]{2,1,0:T(8,128)S(1)}, u32[]{:S(2)}, u32[]{:S(2)}) collective-permute-start(f32[8,32,128]{2,1,0:T(8,128)S(1)} %beams.1.own_beam), channel_id=1, source_target_pairs={{0,8},{8,0},{16,24},{24,16},{1,9},{9,1},{17,25},{25,17},{2,10},{10... | collective-permute-start | bytes 393224 | tf_op jit(solution)/shard_map/ppermute | solution.py:501
  19.2 1.0 copy-start.5
  20.2 0.9 copy-start.6
  81.6 2.0 %collective-permute-start.2 = (bf16[16,128,128]{2,1,0:T(8,128)(2,1)S(1)}, bf16[16,128,128]{2,1,0:T(8,128)(2,1)S(1)}, u32[]{:S(2)}, u32[]{:S(2)}) collective-permute-start(bf16[16,128,128]{2,1,0:T(8,128)(2,1)S(1)} %get-tuple-element.20), channel_id=1, source_target_pairs={{0,8},{8,0},{16,24},{24,16},{1,9},{9,1},{17,25},{25,17},{2,10},{10... | collective-permute-start | bytes 1572872 | tf_op jit(solution)/shard_map/ppermute | solution.py:504
  84.5 19.4 %all-to-all-start.1 = ((bf16[16,128,128]{2,1,0:T(8,128)(2,1)}), bf16[16,128,128]{2,1,0:T(8,128)(2,1)S(1)}, u32[]{:S(2)}, u32[]{:S(2)}) async-start(bf16[16,128,128]{2,1,0:T(8,128)(2,1)} %added.1), calls=%async_computation.1 | async-start | bytes 1048576 | tf_op jit(solution)/shard_map/all_to_all | solution.py:509
